TPU v7x, 512 devices: a whole 4x8x8 slice. The times are simulated.
512 devices in a mesh: dp: 32 (over x, y), mp: 16 (over z, core).
Axes of the slice: x: 4, y: 8, z: 8, core: 2. Of those that a mesh axis runs over, the one named last changes fastest.
Arguments:
- grad_parts: bfloat16 [32, 16384, 1024], P('dp', 'mp'), may hold values from -0.625 to 0.625
- owner: int32 [16], replicated, may hold values from 0 to 15, as said below
- slot: int32 [16], replicated, may hold values from 0 to 2
- left_stat: float32 [48, 1024, 1024], P('mp', 'dp'), may hold values from -6 to 6
- right_stat: float32 [48, 1024, 1024], P('mp', 'dp'), may hold values from -6 to 6
- left_root: bfloat16 [48, 1024, 1024], P('mp', 'dp'), as said below
- right_root: bfloat16 [48, 1024, 1024], P('mp', 'dp'), as said below
Outputs:
- new_left: float32 [48, 1024, 1024], P('mp', 'dp')
- new_right: float32 [48, 1024, 1024], P('mp', 'dp')
- update: bfloat16 [48, 1024, 1024], P('mp', 'dp')
Inputs may be any that keep to these rules, and one draw needn't show every extreme that they name: No two blocks share an owner and a slot; some owner holds 3 blocks; owners 0 and 15 both hold blocks. `left_root`: each slot's matrix is symmetric. `right_root`: each slot's matrix is symmetric.
All inputs are finite; a program needn't handle non-finite values.
Results may differ from a plain program's by a relative error of at most 0.024.
Values may be sent and summed in bfloat16 or wider, within the bound.
No kernel may reach another device: no remote copies, remote signals or barrier semaphores. Data moves between devices by JAX's collectives and lax.ppermute only.
A program may use at most 64 MiB of HBM per device.

v0:
```python
import jax
import jax.numpy as jnp
from jax import lax
from jax.sharding import PartitionSpec as P


def body(grad_parts, owner, slot, left_stat, right_stat, left_root, right_root):
    partial_grad = grad_parts[0]
    summed = lax.psum_scatter(
        partial_grad.astype(jnp.float32).astype(jnp.bfloat16), "dp", scatter_dimension=0, tiled=True
    )
    row_count = summed.shape[0]
    breadth = summed.shape[1]
    slot_count = left_stat.shape[0]
    band_all = lax.all_gather(summed, "mp", axis=0, tiled=True)
    band_all = band_all.reshape(-1, row_count * breadth)
    owner_index = lax.axis_index("mp")
    target = owner * slot_count + slot
    wanted = owner_index * slot_count + jnp.arange(slot_count, dtype=jnp.int32)
    matches = target[None, :] == wanted[:, None]
    filled = jnp.any(matches, axis=1)
    chosen = jnp.dot(matches.astype(jnp.bfloat16), band_all, preferred_element_type=jnp.float32)
    chosen = chosen.astype(jnp.bfloat16).reshape(slot_count, row_count, breadth)
    offset = lax.axis_index("dp") * row_count
    piece = lax.all_gather(chosen, "dp", axis=1, tiled=True)
    crossed = jnp.einsum("srb,snb->srn", chosen, piece, preferred_element_type=jnp.float32)
    left_prod = crossed
    own_cols = lax.dynamic_slice_in_dim(piece, offset, row_count, 2)
    right_prod = jnp.einsum("snr,snb->srb", own_cols, piece, preferred_element_type=jnp.float32)
    left_mix = jnp.einsum("srn,snb->srb", left_root, piece, preferred_element_type=jnp.float32)
    left_prod, right_prod, left_mix = (left_prod, right_prod, left_mix)
    keeper = filled[:, None, None]
    new_left = jnp.where(keeper, 0.95 * left_stat + 0.05 * left_prod, left_stat)
    new_right = jnp.where(keeper, 0.95 * right_stat + 0.05 * right_prod, right_stat)
    mixed = left_mix.astype(jnp.bfloat16)
    columns = jnp.einsum(
        "snb,srb->snr",
        lax.all_gather(mixed, "dp", axis=1, tiled=True),
        right_root,
        preferred_element_type=jnp.float32,
    ).astype(jnp.bfloat16)
    update = lax.all_to_all(columns, "dp", split_axis=1, concat_axis=2, tiled=True)
    return (new_left, new_right, update)


def solution(mesh):
    placed = (
        P("dp", "mp", None),
        P(),
        P(),
        P("mp", "dp", None),
        P("mp", "dp", None),
        P("mp", "dp", None),
        P("mp", "dp", None),
    )
    return jax.shard_map(
        body,
        mesh=mesh,
        in_specs=placed,
        out_specs=(P("mp", "dp", None), P("mp", "dp", None), P("mp", "dp", None)),
        check_vma=False,
    )
```

profile of v0, /device:TPU:1, one launch (start us, length us, event | category | flops | bytes accessed | tf_op | source)
XLA Modules:
  0.0 505.2 jit_solution(16198086519535759258)
XLA Ops:
  7.2 0.0 copy-start
  7.2 0.0 reduce-scatter.2.cloned.1.call-start
  7.2 0.0 copy-start.2
  7.2 0.7 reduce-scatter.2.cloned.1.call-update
  7.9 0.0 all-gather.4.cloned.1.call-start
  8.0 226.0 %reduce-scatter.2.cloned.1.call-done = bf16[32,1024]{1,0:T(8,128)(2,1)} async-done(((bf16[1024,1024]{1,0:T(8,128)(2,1)}), bf16[32,1024]{1,0:T(8,128)(2,1)}) %reduce-scatter.2.cloned.1.call-update) | async-done | bytes 65552 | tf_op jit(solution)/shard_map/reduce_scatter | solution.py:9
  234.0 0.0 all-gather.4.cloned.1.call-update
  234.0 0.0 all-gather.6.cloned.1.call-start
  234.1 0.7 multiply_add_fusion
  234.8 47.7 %all-gather.4.cloned.1.call-done = bf16[512,1024]{1,0:T(8,128)(2,1)} async-done(((bf16[32,1024]{1,0:T(8,128)(2,1)}), bf16[512,1024]{1,0:T(8,128)(2,1)}) %all-gather.4.cloned.1.call-update) | async-done | bytes 1048592 | tf_op jit(solution)/shard_map/all_gather | solution.py:15
  282.4 1.6 reshape.18
  284.0 0.4 convolution_convert_fusion
  284.4 0.8 copy.21
  285.1 0.0 copy-start.1
  285.1 0.0 all-gather.6.cloned.1.call-update
  285.1 0.0 copy-start.4
  285.2 0.0 all-gather.8.cloned.1.call-start
  285.2 92.5 %all-gather.6.cloned.1.call-done = bf16[3,1024,1024]{2,1,0:T(8,128)(2,1)} async-done(((bf16[3,32,1024]{2,1,0:T(8,128)(2,1)}), bf16[3,1024,1024]{2,1,0:T(8,128)(2,1)}) %all-gather.6.cloned.1.call-update) | async-done | bytes 6291472 | tf_op jit(solution)/shard_map/all_gather | solution.py:25
  377.7 0.0 copy-done
  377.7 4.7 fusion.4
  382.3 0.0 all-gather.8.cloned.1.call-update
  382.3 0.2 compare_reduce_fusion
  382.5 0.0 copy-done.2
  382.5 0.0 copy-done.1
  382.5 5.5 %fusion.3 = f32[3,32,1024]{2,1,0:T(8,128)} fusion(f32[3,32,1024]{2,1,0:T(8,128)S(1)} %copy-done.2, bf16[3,32,1024]{2,1,0:T(8,128)(2,1)S(1)} %bitcast.26, bf16[3,1024,1024]{2,1,0:T(8,128)(2,1)} %all-gather.6.cloned.1.call-done, pred[3]{0:T(512)(128)(4,1)S(1)} %compare_reduce_fusion), kind=kOutput, calls=%fused_computation.6 | convolution fusion | flops 201719808 | bytes 7274499 | tf_op jit(solution)/shard_map/srb,snb->srn/dot_general | solution.py:26
  388.1 0.0 copy-start.3
  388.1 85.8 %all-gather.8.cloned.1.call-done = bf16[3,1024,1024]{2,1,0:T(8,128)(2,1)} async-done(((bf16[3,32,1024]{2,1,0:T(8,128)(2,1)}), bf16[3,1024,1024]{2,1,0:T(8,128)(2,1)}) %all-gather.8.cloned.1.call-update) | async-done | bytes 6291472 | tf_op jit(solution)/shard_map/all_gather | solution.py:38
  473.8 0.0 copy-done.4
  473.8 4.7 convolution_convert_fusion.2
  478.5 0.7 copy.16
  479.3 1.4 reshape.20
  480.7 5.7 %all-to-all-start = ((bf16[32,2,1536]{2,1,0:T(2,128)(2,1)}), bf16[32,2,1536]{2,1,0:T(2,128)(2,1)S(1)}, u32[]{:S(2)}, u32[]{:S(2)}) async-start(bf16[32,2,1536]{2,1,0:T(2,128)(2,1)} %reshape.20), calls=%async_computation.1 | async-start | bytes 393216 | tf_op jit(solution)/shard_map/all_to_all | solution.py:42
  486.4 0.0 copy-done.3
  486.4 5.3 %fusion.1 = f32[3,32,1024]{2,1,0:T(8,128)} fusion(f32[3,32,1024]{2,1,0:T(8,128)S(1)} %copy-done.3, bf16[3,1024,1024]{2,1,0:T(8,128)(2,1)} %all-gather.6.cloned.1.call-done, s32[]{:T(128)S(6)} %select_n.11, pred[3]{0:T(512)(128)(4,1)S(1)} %compare_reduce_fusion), kind=kOutput, calls=%fused_computation.3 | convolution fusion | flops 201719808 | bytes 7864327 | tf_op jit(solution)/shard_map/snr,snb->srb/dot_general | solution.py:29
  491.6 4.1 all-to-all-done
  495.8 0.7 reshape.21
  496.5 0.6 copy.17
  497.1 1.5 all_to_all.16
  (1 shorter events, 0.0 us)
Async XLA Ops:
  7.2 370.5 %copy-start = (bf16[3,32,1024]{2,1,0:T(8,128)(2,1)S(1)}, bf16[3,32,1024]{2,1,0:T(8,128)(2,1)}, u32[]{:S(2)}) copy-start(bf16[3,32,1024]{2,1,0:T(8,128)(2,1)} %param.12) | copy-start | bytes 589828
  7.2 226.8 %reduce-scatter.2.cloned.1.call-start = ((), (), s32[]{:S(2)}) async-start(), calls=%async_computation.2 | async-start | bytes 2162688 | tf_op jit(solution)/shard_map/reduce_scatter | solution.py:9
  7.2 375.3 %copy-start.2 = (f32[3,32,1024]{2,1,0:T(8,128)S(1)}, f32[3,32,1024]{2,1,0:T(8,128)}, u32[]{:S(2)}) copy-start(f32[3,32,1024]{2,1,0:T(8,128)} %param.10) | copy-start | bytes 1179652
  7.9 274.5 %all-gather.4.cloned.1.call-start = ((), (), s32[]{:S(2)}) async-start(), calls=%async_computation.3 | async-start | bytes 1114112 | tf_op jit(solution)/shard_map/all_gather | solution.py:15
  234.0 143.6 %all-gather.6.cloned.1.call-start = ((), (), s32[]{:S(2)}) async-start(), calls=%async_computation.4 | async-start | bytes 6488064 | tf_op jit(solution)/shard_map/all_gather | solution.py:25
  285.1 97.4 %copy-start.1 = (bf16[1,3,32,1024]{3,2,1,0:T(8,128)(2,1)S(1)}, bf16[1,3,32,1024]{3,2,1,0:T(8,128)(2,1)}, u32[]{:S(2)}) copy-start(bf16[1,3,32,1024]{3,2,1,0:T(8,128)(2,1)} %copy.21) | copy-start | bytes 589828
  285.1 188.7 %copy-start.4 = (bf16[3,32,1024]{2,1,0:T(8,128)(2,1)S(1)}, bf16[3,32,1024]{2,1,0:T(8,128)(2,1)}, u32[]{:S(2)}) copy-start(bf16[3,32,1024]{2,1,0:T(8,128)(2,1)} %param.13) | copy-start | bytes 589828
  285.2 188.7 %all-gather.8.cloned.1.call-start = ((), (), s32[]{:S(2)}) async-start(), calls=%async_computation.5 | async-start | bytes 6488064 | tf_op jit(solution)/shard_map/all_gather | solution.py:38
  388.1 98.3 %copy-start.3 = (f32[3,32,1024]{2,1,0:T(8,128)S(1)}, f32[3,32,1024]{2,1,0:T(8,128)}, u32[]{:S(2)}) copy-start(f32[3,32,1024]{2,1,0:T(8,128)} %param.11) | copy-start | bytes 1179652
  480.7 15.1 %all-to-all-start = ((bf16[32,2,1536]{2,1,0:T(2,128)(2,1)}), bf16[32,2,1536]{2,1,0:T(2,128)(2,1)S(1)}, u32[]{:S(2)}, u32[]{:S(2)}) async-start(bf16[32,2,1536]{2,1,0:T(2,128)(2,1)} %reshape.20), calls=%async_computation.1 | async-start | bytes 393216 | tf_op jit(solution)/shard_map/all_to_all | solution.py:42
Sparse Core Ops, SparseCore 0:
  12.4 221.5 reduce-scatter.1
  236.3 46.0 all-gather.3
  286.7 90.9 all-gather.5
  382.5 91.2 all-gather.7
where the time goes:
time: 507 us; the launch traced here: 505 us
  waiting for transfers between devices  457 us (90%)
  matrix products  20.5 us (4%)
  between operations  13.9 us (3%)
  local copies, waits for them, and re-layouts  7.29 us (1%)
  starting transfers between devices  5.85 us (1%)
    reduce_scatter x1, waiting for transfers between devices, body(): lax.psum_scatter(partial_grad.astype(jnp.float32).astype(jnp.bfloat16), '...  226 us
    all_gather x1, waiting for transfers between devices, body(): piece = lax.all_gather(chosen, 'dp', axis=1, tiled=True)  92.5 us
    all_gather x1, waiting for transfers between devices, body(): lax.all_gather(mixed, 'dp', axis=1, tiled=True)  85.8 us
    all_gather x1, waiting for transfers between devices, body(): band_all = lax.all_gather(summed, 'mp', axis=0, tiled=True)  47.7 us
  transfers between devices with their start and end apart: 5, of which 5 were waited for; matrix products, arithmetic and copies ran while one was open for 2% of the time, Pallas kernels for 0%

commit v1 on v0

v1 whole, which is shorter than its diff:
```python
import jax
import jax.numpy as jnp
import numpy as np
from jax import lax
from jax.experimental import pallas as pl
from jax.experimental.pallas import tpu as pltpu
from jax.sharding import Mesh
from jax.sharding import PartitionSpec as P

NX, NY, NZ, NC = 4, 8, 8, 2
MP = NZ * NC
F32, BF16 = jnp.float32, jnp.bfloat16


def swap(value, axis):
    return lax.all_to_all(value, axis, 0, 0, tiled=True)


def share(value, axis, size):
    return swap(jnp.broadcast_to(value[None], (size,) + value.shape), axis)


def add_up(value):
    return jnp.sum(value.astype(F32), axis=0).astype(BF16)


def pick_kernel(index_ref, in_ref, out_ref):
    for place in range(out_ref.shape[0]):
        out_ref[place] = in_ref[index_ref[place]]


def pick(index, value):
    return pl.pallas_call(
        pick_kernel,
        out_shape=jax.ShapeDtypeStruct(index.shape + value.shape[1:], value.dtype),
        in_specs=[
            pl.BlockSpec(memory_space=pltpu.SMEM),
            pl.BlockSpec(memory_space=pltpu.VMEM),
        ],
        out_specs=pl.BlockSpec(memory_space=pltpu.VMEM),
    )(index, value)


def body(grad_parts, owner, slot, left_stat, right_stat, left_root, right_root):
    slots, rows, b = left_stat.shape
    ix_panel = b // NX
    here = lax.axis_index("z") * NC + lax.axis_index("c")
    iy = lax.axis_index("y")

    target = owner * slots + slot
    named = target[None, :] == jnp.arange(MP * slots, dtype=jnp.int32)[:, None]
    block_of = jnp.sum(jnp.where(named, jnp.arange(MP, dtype=jnp.int32)[None, :], 0), axis=1)
    filled = jnp.any(target[None, :] == (here * slots + jnp.arange(slots, dtype=jnp.int32))[:, None], axis=1)

    right_full = lax.all_gather(right_root, ("x", "y"), axis=1, tiled=True)

    which = slot[:, None, None]
    offered = jnp.where(
        which == 0, left_root[0][None], jnp.where(which == 1, left_root[1][None], left_root[2][None])
    )
    offered = swap(offered, ("z", "c"))
    root = lax.dynamic_index_in_dim(offered, owner[here], 0, keepdims=False)
    root = swap(root.reshape(rows, NX, ix_panel).transpose(1, 0, 2), "x").reshape(NX * rows, ix_panel)

    part = add_up(swap(grad_parts[0].reshape(NX, ix_panel, b), "x"))
    chunk = add_up(swap(part.reshape(NY, rows, b), "y"))

    panel = share(chunk, "y", NY).reshape(ix_panel, b)
    cross = share(chunk, "x", NX).reshape(NX * rows, b)

    gl = lax.dot_general(cross, panel, (((1,), (1,)), ((), ())), preferred_element_type=F32).astype(BF16)
    own = lax.dynamic_slice_in_dim(panel.reshape(ix_panel, NX, ix_panel), iy * rows, rows, 2)
    own = own.reshape(ix_panel, NX * rows)
    gr = lax.dot_general(own, panel, (((0,), (0,)), ((), ())), preferred_element_type=F32).astype(BF16)
    mx = jnp.dot(root, panel, preferred_element_type=F32).astype(BF16)

    gl = swap(gl.reshape(NX, rows, ix_panel), "x").transpose(1, 0, 2).reshape(rows, b)
    gr = add_up(swap(gr.reshape(NX, rows, b), "x"))
    mx = add_up(swap(mx.reshape(NX, rows, b), "x"))

    cut_rows, cut_cols = 3 * rows // NC, b // NZ
    items = jnp.concatenate([gl, gr, mx], axis=0)
    items = items.reshape(NC, cut_rows, NZ, cut_cols).transpose(2, 0, 1, 3).reshape(MP, cut_rows, cut_cols)
    items = pick(block_of, swap(items, ("z", "c")))
    items = swap(items.reshape(MP, slots, cut_rows, cut_cols), ("z", "c"))
    items = items.reshape(NZ, NC, slots, cut_rows, cut_cols).transpose(2, 1, 3, 0, 4).reshape(slots, 3 * rows, b)
    gl, gr, mx = items[:, :rows], items[:, rows : 2 * rows], items[:, 2 * rows :]

    keeper = filled[:, None, None]
    new_left = jnp.where(keeper, 0.95 * left_stat + 0.05 * gl.astype(F32), left_stat)
    new_right = jnp.where(keeper, 0.95 * right_stat + 0.05 * gr.astype(F32), right_stat)
    update = jnp.einsum("srn,snb->srb", mx, right_full, preferred_element_type=F32)
    update = jnp.where(keeper, update, 0.0).astype(BF16)
    return new_left, new_right, update


def solution(mesh):
    grid = Mesh(np.asarray(mesh.devices).reshape(NX, NY, NZ, NC), ("x", "y", "z", "c"))
    dp, mp = ("x", "y"), ("z", "c")
    state = P(mp, dp, None)
    return jax.shard_map(
        body,
        mesh=grid,
        in_specs=(P(dp, mp, None), P(), P(), state, state, state, state),
        out_specs=(state, state, state),
        check_vma=False,
    )
```

time: 507 us -> 228 us (0.45)
  waiting for transfers between devices: 457 us -> 104 us
  starting transfers between devices: 5.85 us -> 53.7 us
  blocking collectives: 0 us -> 33.9 us
  matrix products: 20.5 us -> 7.48 us
    reduce_scatter x1 -> x0, waiting for transfers between devices: 226 us -> none  [body(): lax.psum_scatter(partial_grad.astype(jnp.float32).astype(jnp.bfloat16), '...]
    all_gather x3 -> x1, waiting for transfers between devices: 226 us -> 0.01 us  [body(): right_full = lax.all_gather(right_root, ('x', 'y'), axis=1, tiled=True)]
    all_to_all x1 -> x9, waiting for transfers between devices: 4.14 us -> 104 us  [swap(): return lax.all_to_all(value, axis, 0, 0, tiled=True)]
    all_to_all x1 -> x9, starting transfers between devices: 5.7 us -> 53.7 us  [swap(): return lax.all_to_all(value, axis, 0, 0, tiled=True)]
    all_to_all x0 -> x2, blocking collectives: none -> 33.9 us  [swap(): return lax.all_to_all(value, axis, 0, 0, tiled=True)]
    dot_general x5 -> x4, matrix products: 20.5 us -> 7.48 us  [the longest x1 4.65 us: body(): jnp.einsum('srn,snb->srb', mx, right_full, preferred_element_type=F32)]
  transfers between devices with their start and end apart: 5 -> 10, of which waited for: 5 -> 9; matrix products, arithmetic and copies ran while one was open for 2% -> 5% of each run, Pallas kernels for 0% -> 1%
where the time goes in v1:
time: 228 us; the launch traced here: 227 us
  waiting for transfers between devices  104 us (46%)
  starting transfers between devices  53.7 us (24%)
  blocking collectives  33.9 us (15%)
  between operations  16.2 us (7%)
  matrix products  7.48 us (3%)
  local copies, waits for them, and re-layouts  4.83 us (2%)
  other arithmetic  4.53 us (2%)
    all_to_all x9, waiting for transfers between devices, swap(): return lax.all_to_all(value, axis, 0, 0, tiled=True)  104 us
    all_to_all x9, starting transfers between devices, swap(): return lax.all_to_all(value, axis, 0, 0, tiled=True)  53.7 us
    all_to_all x2, blocking collectives, swap(): return lax.all_to_all(value, axis, 0, 0, tiled=True)  33.9 us
    dot_general x1, matrix products, body(): jnp.einsum('srn,snb->srb', mx, right_full, preferred_element_type=F32)  4.65 us
  transfers between devices with their start and end apart: 10, of which 9 were waited for; matrix products, arithmetic and copies ran while one was open for 5% of the time, Pallas kernels for 1%

profile of v1, /device:TPU:1, one launch (start us, length us, event | category | flops | bytes accessed | tf_op | source)
XLA Modules:
  0.0 226.9 jit_solution(978864557889700676)
XLA Ops:
  7.2 0.0 copy-start.4
  7.2 0.0 copy-start.3
  7.2 0.0 all-gather.2.cloned.1.call-start
  7.2 0.7 all-gather.2.cloned.1.call-update
  7.9 25.3 %all_to_all.55 = bf16[4,256,1024]{2,1,0:T(8,128)(2,1)S(1)} all-to-all(bf16[4,256,1024]{2,1,0:T(8,128)(2,1)} %bitcast.49), channel_id=1, replica_groups=mesh['x'=4,'y'=8,'z'=8,'c'=2] {'x'}, dimensions={0} | all-to-all | bytes 4194304 | tf_op jit(solution)/shard_map/all_to_all | solution.py:16
  33.2 1.3 reduce_sum.58
  34.5 12.9 %all-to-all-start.1 = ((bf16[8,32,1024]{2,1,0:T(8,128)(2,1)}), bf16[8,32,1024]{2,1,0:T(8,128)(2,1)S(1)}, u32[]{:S(2)}, u32[]{:S(2)}) async-start(bf16[8,32,1024]{2,1,0:T(8,128)(2,1)} %bitcast.1), calls=%async_computation.1 | async-start | bytes 1048576 | tf_op jit(solution)/shard_map/all_to_all | solution.py:16
  47.5 0.0 copy-done.4
  47.5 1.2 select_select_fusion
  48.7 17.2 %all-to-all-done.1 = bf16[8,32,1024]{2,1,0:T(8,128)(2,1)S(1)} async-done(((bf16[8,32,1024]{2,1,0:T(8,128)(2,1)}), bf16[8,32,1024]{2,1,0:T(8,128)(2,1)S(1)}, u32[]{:S(2)}, u32[]{:S(2)}) %all-to-all-start.1) | async-done | bytes 524320 | tf_op jit(solution)/shard_map/all_to_all | solution.py:16
  65.9 11.6 %all-to-all-start.6 = ((bf16[16,32,1024]{2,1,0:T(8,128)(2,1)}), bf16[16,32,1024]{2,1,0:T(8,128)(2,1)S(1)}, u32[]{:S(2)}, u32[]{:S(2)}) async-start(bf16[16,32,1024]{2,1,0:T(8,128)(2,1)} %select_select_fusion), calls=%async_computation.6 | async-start | bytes 2097152 | tf_op jit(solution)/shard_map/all_to_all | solution.py:16
  77.5 0.1 reduce_sum.59
  77.6 27.9 %all-to-all-done.6 = bf16[16,32,1024]{2,1,0:T(8,128)(2,1)S(1)} async-done(((bf16[16,32,1024]{2,1,0:T(8,128)(2,1)}), bf16[16,32,1024]{2,1,0:T(8,128)(2,1)S(1)}, u32[]{:S(2)}, u32[]{:S(2)}) %all-to-all-start.6) | async-done | bytes 1048608 | tf_op jit(solution)/shard_map/all_to_all | solution.py:16
  105.5 8.6 %all_to_all.56 = bf16[4,32,1024]{2,1,0:T(8,128)(2,1)S(1)} all-to-all(bf16[4,32,1024]{2,1,0:T(8,128)(2,1)S(1)} %broadcast_in_dim.101), channel_id=1, replica_groups=mesh['x'=4,'y'=8,'z'=8,'c'=2] {'x'}, dimensions={0} | all-to-all | bytes 524288 | tf_op jit(solution)/shard_map/all_to_all | solution.py:16
  114.1 0.9 broadcast_in_dim.102
  115.0 3.5 %all-to-all-start.3 = ((bf16[8,32,1024]{2,1,0:T(8,128)(2,1)}), bf16[8,32,1024]{2,1,0:T(8,128)(2,1)S(1)}, u32[]{:S(2)}, u32[]{:S(2)}) async-start(bf16[8,32,1024]{2,1,0:T(8,128)(2,1)} %broadcast_in_dim.102), calls=%async_computation.3 | async-start | bytes 1048576 | tf_op jit(solution)/shard_map/all_to_all | solution.py:16
  118.5 0.6 dynamic_slice.11
  121.1 0.6 copy.27
  121.7 14.7 %all-to-all-done.3 = bf16[8,32,1024]{2,1,0:T(8,128)(2,1)S(1)} async-done(((bf16[8,32,1024]{2,1,0:T(8,128)(2,1)}), bf16[8,32,1024]{2,1,0:T(8,128)(2,1)S(1)}, u32[]{:S(2)}, u32[]{:S(2)}) %all-to-all-start.3) | async-done | bytes 524320 | tf_op jit(solution)/shard_map/all_to_all | solution.py:16
  136.4 3.3 %all-to-all-start.7 = ((bf16[4,32,256]{2,1,0:T(8,128)(2,1)}), bf16[4,32,256]{2,1,0:T(8,128)(2,1)S(1)}, u32[]{:S(2)}, u32[]{:S(2)}) async-start(bf16[4,32,256]{2,1,0:T(8,128)(2,1)} %copy.27), calls=%async_computation.7 | async-start | bytes 131072 | tf_op jit(solution)/shard_map/all_to_all | solution.py:16
  139.7 0.0 copy-start.1
  139.7 0.0 copy-start.2
  139.7 0.9 convolution_convert_fusion.2
  140.7 0.4 reshape_reshape.3
  141.1 3.1 %all-to-all-done.7 = bf16[4,32,256]{2,1,0:T(8,128)(2,1)S(1)} async-done(((bf16[4,32,256]{2,1,0:T(8,128)(2,1)}), bf16[4,32,256]{2,1,0:T(8,128)(2,1)S(1)}, u32[]{:S(2)}, u32[]{:S(2)}) %all-to-all-start.7) | async-done | bytes 65568 | tf_op jit(solution)/shard_map/all_to_all | solution.py:16
  144.2 3.3 %all-to-all-start.4 = ((bf16[4,32,256]{2,1,0:T(8,128)(2,1)}), bf16[4,32,256]{2,1,0:T(8,128)(2,1)S(1)}, u32[]{:S(2)}, u32[]{:S(2)}) async-start(bf16[4,32,256]{2,1,0:T(8,128)(2,1)} %bitcast.4), calls=%async_computation.4 | async-start | bytes 131072 | tf_op jit(solution)/shard_map/all_to_all | solution.py:16
  147.5 0.9 convolution_convert_fusion
  148.4 0.2 constant_dynamic-slice_fusion
  148.6 0.1 copy.26
  148.7 3.1 %all-to-all-done.4 = bf16[4,32,256]{2,1,0:T(8,128)(2,1)S(1)} async-done(((bf16[4,32,256]{2,1,0:T(8,128)(2,1)}), bf16[4,32,256]{2,1,0:T(8,128)(2,1)S(1)}, u32[]{:S(2)}, u32[]{:S(2)}) %all-to-all-start.4) | async-done | bytes 65568 | tf_op jit(solution)/shard_map/all_to_all | solution.py:16
  151.9 3.4 %all-to-all-start.8 = ((bf16[4,32,1024]{2,1,0:T(8,128)(2,1)}), bf16[4,32,1024]{2,1,0:T(8,128)(2,1)S(1)}, u32[]{:S(2)}, u32[]{:S(2)}) async-start(bf16[4,32,1024]{2,1,0:T(8,128)(2,1)} %bitcast.14), calls=%async_computation.8 | async-start | bytes 524288 | tf_op jit(solution)/shard_map/all_to_all | solution.py:16
  155.3 0.9 convolution_convert_fusion.1
  156.3 4.6 %all-to-all-done.8 = bf16[4,32,1024]{2,1,0:T(8,128)(2,1)S(1)} async-done(((bf16[4,32,1024]{2,1,0:T(8,128)(2,1)}), bf16[4,32,1024]{2,1,0:T(8,128)(2,1)S(1)}, u32[]{:S(2)}, u32[]{:S(2)}) %all-to-all-start.8) | async-done | bytes 262176 | tf_op jit(solution)/shard_map/all_to_all | solution.py:16
  160.8 3.4 %all-to-all-start.5 = ((bf16[4,32,1024]{2,1,0:T(8,128)(2,1)}), bf16[4,32,1024]{2,1,0:T(8,128)(2,1)S(1)}, u32[]{:S(2)}, u32[]{:S(2)}) async-start(bf16[4,32,1024]{2,1,0:T(8,128)(2,1)} %bitcast.7), calls=%async_computation.5 | async-start | bytes 524288 | tf_op jit(solution)/shard_map/all_to_all | solution.py:16
  164.3 5.4 %all-to-all-done.5 = bf16[4,32,1024]{2,1,0:T(8,128)(2,1)S(1)} async-done(((bf16[4,32,1024]{2,1,0:T(8,128)(2,1)}), bf16[4,32,1024]{2,1,0:T(8,128)(2,1)S(1)}, u32[]{:S(2)}, u32[]{:S(2)}) %all-to-all-start.5) | async-done | bytes 262176 | tf_op jit(solution)/shard_map/all_to_all | solution.py:16
  169.8 0.7 copy.28
  170.5 8.7 %all-to-all-start.9 = ((bf16[16,48,128]{2,1,0:T(8,128)(2,1)}), bf16[16,48,128]{2,1,0:T(8,128)(2,1)S(1)}, u32[]{:S(2)}, u32[]{:S(2)}) async-start(bf16[16,48,128]{2,1,0:T(8,128)(2,1)} %bitcast.16), calls=%async_computation.9 | async-start | bytes 393216 | tf_op jit(solution)/shard_map/all_to_all | solution.py:16
  179.3 0.6 select_reduce_fusion.index_ref
  179.9 9.7 %all-to-all-done.9.in_ref = bf16[16,48,128]{2,1,0:T(8,128)(2,1)S(1)} async-done(((bf16[16,48,128]{2,1,0:T(8,128)(2,1)}), bf16[16,48,128]{2,1,0:T(8,128)(2,1)S(1)}, u32[]{:S(2)}, u32[]{:S(2)}) %all-to-all-start.9) | async-done | bytes 196640 | tf_op jit(solution)/shard_map/all_to_all | solution.py:16
  189.6 0.7 copy-done
  190.3 1.8 shard_map.94
  192.1 3.5 %all-to-all-start.10 = ((bf16[16,3,48,128]{3,2,1,0:T(8,128)(2,1)}), bf16[16,3,48,128]{3,2,1,0:T(8,128)(2,1)S(1)}, u32[]{:S(2)}, u32[]{:S(2)}) async-start(bf16[16,3,48,128]{3,2,1,0:T(8,128)(2,1)} %bitcast.47), calls=%async_computation.10 | async-start | bytes 1179648 | tf_op jit(solution)/shard_map/all_to_all | solution.py:16
  195.6 0.2 compare_reduce_fusion
  195.8 18.1 %all-to-all-done.10 = bf16[16,3,48,128]{3,2,1,0:T(8,128)(2,1)S(1)} async-done(((bf16[16,3,48,128]{3,2,1,0:T(8,128)(2,1)}), bf16[16,3,48,128]{3,2,1,0:T(8,128)(2,1)S(1)}, u32[]{:S(2)}, u32[]{:S(2)}) %all-to-all-start.10) | async-done | bytes 589856 | tf_op jit(solution)/shard_map/all_to_all | solution.py:16
  213.9 0.2 copy.33
  214.1 0.3 reshape.77
  214.4 1.1 add_select_fusion
  215.4 4.7 %fusion = bf16[3,32,1024]{2,1,0:T(8,128)(2,1)} fusion(bf16[3,1024,1024]{2,1,0:T(8,128)(2,1)} %all-gather.2.cloned.1.call-done, bf16[3,96,1024]{2,1,0:T(8,128)(2,1)S(1)} %reshape.77, pred[3]{0:T(512)(128)(4,1)S(1)} %compare_reduce_fusion), kind=kOutput, calls=%fused_computation.3 | convolution fusion | flops 201523200 | bytes 6685184 | tf_op jit(solution)/shard_map/srn,snb->srb/dot_general | solution.py:92
  (20 shorter events, 0.3 us)
Async XLA Ops:
  7.2 40.3 %copy-start.4 = (s32[16]{0:T(128)S(1)}, s32[16]{0:T(128)}, u32[]{:S(2)}) copy-start(s32[16]{0:T(128)} %param.9) | copy-start | bytes 196
  7.2 40.3 %copy-start.3 = (bf16[3,32,1024]{2,1,0:T(8,128)(2,1)S(1)}, bf16[3,32,1024]{2,1,0:T(8,128)(2,1)}, u32[]{:S(2)}) copy-start(bf16[3,32,1024]{2,1,0:T(8,128)(2,1)} %param.12) | copy-start | bytes 589828
  7.2 208.3 %all-gather.2.cloned.1.call-start = ((), (), s32[]{:S(2)}) async-start(), calls=%async_computation.11 | async-start | bytes 6488064 | tf_op jit(solution)/shard_map/all_gather | solution.py:55
  33.2 85.2 %copy-start.5 = (s32[16]{0:T(128)S(1)}, s32[16]{0:T(128)}, u32[]{:S(2)}) copy-start(s32[16]{0:T(128)} %param.8) | copy-start | bytes 196
  34.5 31.4 %all-to-all-start.1 = ((bf16[8,32,1024]{2,1,0:T(8,128)(2,1)}), bf16[8,32,1024]{2,1,0:T(8,128)(2,1)S(1)}, u32[]{:S(2)}, u32[]{:S(2)}) async-start(bf16[8,32,1024]{2,1,0:T(8,128)(2,1)} %bitcast.1), calls=%async_computation.1 | async-start | bytes 1048576 | tf_op jit(solution)/shard_map/all_to_all | solution.py:16
  65.9 39.6 %all-to-all-start.6 = ((bf16[16,32,1024]{2,1,0:T(8,128)(2,1)}), bf16[16,32,1024]{2,1,0:T(8,128)(2,1)S(1)}, u32[]{:S(2)}, u32[]{:S(2)}) async-start(bf16[16,32,1024]{2,1,0:T(8,128)(2,1)} %select_select_fusion), calls=%async_computation.6 | async-start | bytes 2097152 | tf_op jit(solution)/shard_map/all_to_all | solution.py:16
  115.0 21.5 %all-to-all-start.3 = ((bf16[8,32,1024]{2,1,0:T(8,128)(2,1)}), bf16[8,32,1024]{2,1,0:T(8,128)(2,1)S(1)}, u32[]{:S(2)}, u32[]{:S(2)}) async-start(bf16[8,32,1024]{2,1,0:T(8,128)(2,1)} %broadcast_in_dim.102), calls=%async_computation.3 | async-start | bytes 1048576 | tf_op jit(solution)/shard_map/all_to_all | solution.py:16
  136.4 7.7 %all-to-all-start.7 = ((bf16[4,32,256]{2,1,0:T(8,128)(2,1)}), bf16[4,32,256]{2,1,0:T(8,128)(2,1)S(1)}, u32[]{:S(2)}, u32[]{:S(2)}) async-start(bf16[4,32,256]{2,1,0:T(8,128)(2,1)} %copy.27), calls=%async_computation.7 | async-start | bytes 131072 | tf_op jit(solution)/shard_map/all_to_all | solution.py:16
  139.7 74.6 %copy-start.1 = (f32[3,32,1024]{2,1,0:T(8,128)S(1)}, f32[3,32,1024]{2,1,0:T(8,128)}, u32[]{:S(2)}) copy-start(f32[3,32,1024]{2,1,0:T(8,128)} %param.11) | copy-start | bytes 1179652
  139.7 74.6 %copy-start.2 = (f32[3,32,1024]{2,1,0:T(8,128)S(1)}, f32[3,32,1024]{2,1,0:T(8,128)}, u32[]{:S(2)}) copy-start(f32[3,32,1024]{2,1,0:T(8,128)} %param.10) | copy-start | bytes 1179652
  144.2 7.7 %all-to-all-start.4 = ((bf16[4,32,256]{2,1,0:T(8,128)(2,1)}), bf16[4,32,256]{2,1,0:T(8,128)(2,1)S(1)}, u32[]{:S(2)}, u32[]{:S(2)}) async-start(bf16[4,32,256]{2,1,0:T(8,128)(2,1)} %bitcast.4), calls=%async_computation.4 | async-start | bytes 131072 | tf_op jit(solution)/shard_map/all_to_all | solution.py:16
  151.9 8.9 %all-to-all-start.8 = ((bf16[4,32,1024]{2,1,0:T(8,128)(2,1)}), bf16[4,32,1024]{2,1,0:T(8,128)(2,1)S(1)}, u32[]{:S(2)}, u32[]{:S(2)}) async-start(bf16[4,32,1024]{2,1,0:T(8,128)(2,1)} %bitcast.14), calls=%async_computation.8 | async-start | bytes 524288 | tf_op jit(solution)/shard_map/all_to_all | solution.py:16
  160.8 8.9 %all-to-all-start.5 = ((bf16[4,32,1024]{2,1,0:T(8,128)(2,1)}), bf16[4,32,1024]{2,1,0:T(8,128)(2,1)S(1)}, u32[]{:S(2)}, u32[]{:S(2)}) async-start(bf16[4,32,1024]{2,1,0:T(8,128)(2,1)} %bitcast.7), calls=%async_computation.5 | async-start | bytes 524288 | tf_op jit(solution)/shard_map/all_to_all | solution.py:16
  170.5 19.1 %all-to-all-start.9 = ((bf16[16,48,128]{2,1,0:T(8,128)(2,1)}), bf16[16,48,128]{2,1,0:T(8,128)(2,1)S(1)}, u32[]{:S(2)}, u32[]{:S(2)}) async-start(bf16[16,48,128]{2,1,0:T(8,128)(2,1)} %bitcast.16), calls=%async_computation.9 | async-start | bytes 393216 | tf_op jit(solution)/shard_map/all_to_all | solution.py:16
  189.6 0.7 copy-start
  192.1 21.8 %all-to-all-start.10 = ((bf16[16,3,48,128]{3,2,1,0:T(8,128)(2,1)}), bf16[16,3,48,128]{3,2,1,0:T(8,128)(2,1)S(1)}, u32[]{:S(2)}, u32[]{:S(2)}) async-start(bf16[16,3,48,128]{3,2,1,0:T(8,128)(2,1)} %bitcast.47), calls=%async_computation.10 | async-start | bytes 1179648 | tf_op jit(solution)/shard_map/all_to_all | solution.py:16
Sparse Core Ops, SparseCore 0:
  11.2 102.0 all-gather.1

commit v2 on v1

--- a/solution.py
+++ b/solution.py
@@ -52,39 +52,37 @@
     block_of = jnp.sum(jnp.where(named, jnp.arange(MP, dtype=jnp.int32)[None, :], 0), axis=1)
     filled = jnp.any(target[None, :] == (here * slots + jnp.arange(slots, dtype=jnp.int32))[:, None], axis=1)
 
-    right_full = lax.all_gather(right_root, ("x", "y"), axis=1, tiled=True)
-
-    which = slot[:, None, None]
-    offered = jnp.where(
-        which == 0, left_root[0][None], jnp.where(which == 1, left_root[1][None], left_root[2][None])
-    )
-    offered = swap(offered, ("z", "c"))
-    root = lax.dynamic_index_in_dim(offered, owner[here], 0, keepdims=False)
-    root = swap(root.reshape(rows, NX, ix_panel).transpose(1, 0, 2), "x").reshape(NX * rows, ix_panel)
+    left_all = lax.all_gather(left_root, ("z", "c"), axis=0)
+    root = lax.dynamic_slice(left_all, (owner[here], slot[here], 0, 0), (1, 1, rows, b)).reshape(rows, NX, ix_panel)
 
     part = add_up(swap(grad_parts[0].reshape(NX, ix_panel, b), "x"))
+    right_root, part = lax.optimization_barrier((right_root, part))
+    right_full = lax.all_gather(right_root, ("x", "y"), axis=1, tiled=True)
     chunk = add_up(swap(part.reshape(NY, rows, b), "y"))
 
     panel = share(chunk, "y", NY).reshape(ix_panel, b)
-    cross = share(chunk, "x", NX).reshape(NX * rows, b)
+    cross = jnp.broadcast_to(chunk[None], (NX, rows, b))
+    cross = swap(jnp.concatenate([cross, root.transpose(1, 0, 2)], axis=2), "x")
+    cross, root = cross[:, :, :b].reshape(NX * rows, b), cross[:, :, b:]
 
+    own = lax.dynamic_slice_in_dim(panel.reshape(ix_panel, NX, ix_panel), iy * rows, rows, 2)
+    own = own.transpose(1, 2, 0)
+    lhs = jnp.concatenate([own, root], axis=1).reshape(2 * NX * rows, ix_panel)
+    both = jnp.dot(lhs, panel, preferred_element_type=F32).astype(BF16).reshape(NX, 2 * rows, b)
     gl = lax.dot_general(cross, panel, (((1,), (1,)), ((), ())), preferred_element_type=F32).astype(BF16)
-    own = lax.dynamic_slice_in_dim(panel.reshape(ix_panel, NX, ix_panel), iy * rows, rows, 2)
-    own = own.reshape(ix_panel, NX * rows)
-    gr = lax.dot_general(own, panel, (((0,), (0,)), ((), ())), preferred_element_type=F32).astype(BF16)
-    mx = jnp.dot(root, panel, preferred_element_type=F32).astype(BF16)
-
-    gl = swap(gl.reshape(NX, rows, ix_panel), "x").transpose(1, 0, 2).reshape(rows, b)
-    gr = add_up(swap(gr.reshape(NX, rows, b), "x"))
-    mx = add_up(swap(mx.reshape(NX, rows, b), "x"))
+    half = ix_panel // 2
+    gl = gl.reshape(NX, rows, 2, half).transpose(0, 2, 1, 3).reshape(NX, 2 * rows, half)
+    both = swap(jnp.concatenate([both, gl], axis=2), "x")
+    gl = both[:, :, b:].reshape(NX, 2, rows, half).transpose(2, 0, 1, 3).reshape(rows, b)
+    both = add_up(both[:, :, :b])
 
     cut_rows, cut_cols = 3 * rows // NC, b // NZ
-    items = jnp.concatenate([gl, gr, mx], axis=0)
+    items = jnp.concatenate([both, gl], axis=0)
     items = items.reshape(NC, cut_rows, NZ, cut_cols).transpose(2, 0, 1, 3).reshape(MP, cut_rows, cut_cols)
     items = pick(block_of, swap(items, ("z", "c")))
     items = swap(items.reshape(MP, slots, cut_rows, cut_cols), ("z", "c"))
     items = items.reshape(NZ, NC, slots, cut_rows, cut_cols).transpose(2, 1, 3, 0, 4).reshape(slots, 3 * rows, b)
-    gl, gr, mx = items[:, :rows], items[:, rows : 2 * rows], items[:, 2 * rows :]
+    gr, mx, gl = items[:, :rows], items[:, rows : 2 * rows], items[:, 2 * rows :]
 
     keeper = filled[:, None, None]
     new_left = jnp.where(keeper, 0.95 * left_stat + 0.05 * gl.astype(F32), left_stat)

time: 228 us -> 167 us (0.73)
  waiting for transfers between devices: 104 us -> 41.6 us
  blocking collectives: 33.9 us -> 61.2 us
  starting transfers between devices: 53.7 us -> 28.6 us
    all_to_all x9 -> x4, waiting for transfers between devices: 104 us -> 40.3 us  [swap(): return lax.all_to_all(value, axis, 0, 0, tiled=True)]
    all_to_all x2 -> x3, blocking collectives: 33.9 us -> 61.2 us  [swap(): return lax.all_to_all(value, axis, 0, 0, tiled=True)]
    all_to_all x9 -> x4, starting transfers between devices: 53.7 us -> 28.6 us  [swap(): return lax.all_to_all(value, axis, 0, 0, tiled=True)]
  transfers between devices with their start and end apart: 10 -> 6, of which waited for: 9 -> 5; matrix products, arithmetic and copies ran while one was open for 5% -> 6% of each run, Pallas kernels for 1% -> 1%
where the time goes in v2:
time: 167 us; the launch traced here: 166 us
  blocking collectives  61.2 us (37%)
  waiting for transfers between devices  41.6 us (25%)
  starting transfers between devices  28.6 us (17%)
  between operations  18.2 us (11%)
  local copies, waits for them, and re-layouts  5.95 us (4%)
  matrix products  5.28 us (3%)
  other arithmetic  3.62 us (2%)
  Pallas kernels  1.82 us (1%)
    all_to_all x3, blocking collectives, swap(): return lax.all_to_all(value, axis, 0, 0, tiled=True)  61.2 us
    all_to_all x4, waiting for transfers between devices, swap(): return lax.all_to_all(value, axis, 0, 0, tiled=True)  40.3 us
    all_to_all x4, starting transfers between devices, swap(): return lax.all_to_all(value, axis, 0, 0, tiled=True)  28.6 us
    dot_general x1, matrix products, body(): jnp.einsum('srn,snb->srb', mx, right_full, preferred_element_type=F32)  4.66 us
  transfers between devices with their start and end apart: 6, of which 5 were waited for; matrix products, arithmetic and copies ran while one was open for 6% of the time, Pallas kernels for 1%

profile of v2, /device:TPU:1, one launch (start us, length us, event | category | flops | bytes accessed | tf_op | source)
XLA Modules:
  0.0 166.2 jit_solution(7870926960114082638)
XLA Ops:
  7.2 0.0 all-gather.6.cloned.1.call-start
  7.2 0.7 all-gather.6.cloned.1.call-update
  7.9 0.0 all-gather.4.cloned.1.call-start
  7.9 25.3 %all_to_all.35 = bf16[4,256,1024]{2,1,0:T(8,128)(2,1)S(1)} all-to-all(bf16[4,256,1024]{2,1,0:T(8,128)(2,1)} %bitcast.45), channel_id=1, replica_groups=mesh['x'=4,'y'=8,'z'=8,'c'=2] {'x'}, dimensions={0} | all-to-all | bytes 4194304 | tf_op jit(solution)/shard_map/all_to_all | solution.py:16
  33.3 0.4 reduce_sum.46
  33.7 0.0 all-gather.4.cloned.1.call-update
  33.7 26.2 %all_to_all.36 = bf16[8,32,1024]{2,1,0:T(8,128)(2,1)S(1)} all-to-all(bf16[8,32,1024]{2,1,0:T(8,128)(2,1)S(1)} %bitcast.47), channel_id=1, replica_groups=mesh['x'=4,'y'=8,'z'=8,'c'=2] {'y'}, dimensions={0} | all-to-all | bytes 1048576 | tf_op jit(solution)/shard_map/all_to_all | solution.py:16
  59.9 0.1 reduce_sum.47
  60.0 0.8 broadcast_in_dim.54
  60.8 3.5 %all-to-all-start.2 = ((bf16[8,32,1024]{2,1,0:T(8,128)(2,1)}), bf16[8,32,1024]{2,1,0:T(8,128)(2,1)S(1)}, u32[]{:S(2)}, u32[]{:S(2)}) async-start(bf16[8,32,1024]{2,1,0:T(8,128)(2,1)} %broadcast_in_dim.54), calls=%async_computation.2 | async-start | bytes 1048576 | tf_op jit(solution)/shard_map/all_to_all | solution.py:16
  64.3 0.0 copy-done.4
  64.3 0.6 dynamic_slice.13
  66.2 0.0 copy-done.3
  66.2 0.6 dynamic_slice.14
  69.4 0.0 all-gather.6.cloned.1.call-done
  69.4 0.9 constant_dynamic-slice_fusion
  70.4 0.7 pad_maximum_fusion.1
  71.1 6.8 %all-to-all-done.2 = bf16[8,32,1024]{2,1,0:T(8,128)(2,1)S(1)} async-done(((bf16[8,32,1024]{2,1,0:T(8,128)(2,1)}), bf16[8,32,1024]{2,1,0:T(8,128)(2,1)S(1)}, u32[]{:S(2)}, u32[]{:S(2)}) %all-to-all-start.2) | async-done | bytes 524320 | tf_op jit(solution)/shard_map/all_to_all | solution.py:16
  78.0 3.5 %all-to-all-start.3 = ((bf16[4,32,1280]{2,1,0:T(8,128)(2,1)}), bf16[4,32,1280]{2,1,0:T(8,128)(2,1)S(1)}, u32[]{:S(2)}, u32[]{:S(2)}) async-start(bf16[4,32,1280]{2,1,0:T(8,128)(2,1)} %pad_maximum_fusion.1), calls=%async_computation.3 | async-start | bytes 655360 | tf_op jit(solution)/shard_map/all_to_all | solution.py:16
  81.4 0.4 reshape_reshape.3
  81.8 0.2 dynamic-slice_bitcast_fusion
  82.0 5.6 %all-to-all-done.3 = bf16[4,32,1280]{2,1,0:T(8,128)(2,1)S(1)} async-done(((bf16[4,32,1280]{2,1,0:T(8,128)(2,1)}), bf16[4,32,1280]{2,1,0:T(8,128)(2,1)S(1)}, u32[]{:S(2)}, u32[]{:S(2)}) %all-to-all-start.3) | async-done | bytes 327712 | tf_op jit(solution)/shard_map/all_to_all | solution.py:16
  87.7 0.2 copy.40
  87.9 0.4 pad_maximum_fusion.2
  88.2 0.2 copy.35
  88.4 0.3 convolution_convert_fusion.1
  88.8 0.3 convolution_convert_fusion
  89.1 0.1 pad_maximum_fusion
  89.2 9.7 %all_to_all.37 = bf16[4,64,1152]{2,1,0:T(8,128)(2,1)S(1)} all-to-all(bf16[4,64,1152]{2,1,0:T(8,128)(2,1)S(1)} %pad_maximum_fusion), channel_id=1, replica_groups=mesh['x'=4,'y'=8,'z'=8,'c'=2] {'x'}, dimensions={0} | all-to-all | bytes 1179648 | tf_op jit(solution)/shard_map/all_to_all | solution.py:16
  98.8 0.1 copy.37
  98.9 0.1 slice_reduce_fusion
  99.0 0.0 copy-start.1
  99.0 0.0 copy-start.2
  99.1 0.7 copy.38
  99.8 18.1 %all-to-all-start.5 = ((bf16[16,48,128]{2,1,0:T(8,128)(2,1)}), bf16[16,48,128]{2,1,0:T(8,128)(2,1)S(1)}, u32[]{:S(2)}, u32[]{:S(2)}) async-start(bf16[16,48,128]{2,1,0:T(8,128)(2,1)} %bitcast.16), calls=%async_computation.5 | async-start | bytes 393216 | tf_op jit(solution)/shard_map/all_to_all | solution.py:16
  118.0 0.6 select_reduce_fusion.index_ref
  118.6 9.7 %all-to-all-done.5.in_ref = bf16[16,48,128]{2,1,0:T(8,128)(2,1)S(1)} async-done(((bf16[16,48,128]{2,1,0:T(8,128)(2,1)}), bf16[16,48,128]{2,1,0:T(8,128)(2,1)S(1)}, u32[]{:S(2)}, u32[]{:S(2)}) %all-to-all-start.5) | async-done | bytes 196640 | tf_op jit(solution)/shard_map/all_to_all | solution.py:16
  128.3 0.7 copy-done
  129.0 1.8 %shard_map.94 = bf16[48,48,128]{2,1,0:T(8,128)(2,1)} custom-call(s32[48]{0:T(128)} %select_reduce_fusion.index_ref, bf16[16,48,128]{2,1,0:T(8,128)(2,1)} %copy-done), custom_call_target="tpu_custom_call" | custom-call | tf_op jit(solution)/shard_map/pallas_call | solution.py:33
  130.8 3.5 %all-to-all-start.6 = ((bf16[16,3,48,128]{3,2,1,0:T(8,128)(2,1)}), bf16[16,3,48,128]{3,2,1,0:T(8,128)(2,1)S(1)}, u32[]{:S(2)}, u32[]{:S(2)}) async-start(bf16[16,3,48,128]{3,2,1,0:T(8,128)(2,1)} %bitcast.43), calls=%async_computation.6 | async-start | bytes 1179648 | tf_op jit(solution)/shard_map/all_to_all | solution.py:16
  134.3 0.2 compare_reduce_fusion
  134.5 18.1 %all-to-all-done.6 = bf16[16,3,48,128]{3,2,1,0:T(8,128)(2,1)S(1)} async-done(((bf16[16,3,48,128]{3,2,1,0:T(8,128)(2,1)}), bf16[16,3,48,128]{3,2,1,0:T(8,128)(2,1)S(1)}, u32[]{:S(2)}, u32[]{:S(2)}) %all-to-all-start.6) | async-done | bytes 589856 | tf_op jit(solution)/shard_map/all_to_all | solution.py:16
  152.6 0.2 copy.43
  152.8 0.3 reshape.72
  153.1 0.0 copy-done.1
  153.1 1.1 add_select_fusion
  154.2 0.6 all-gather.4.cloned.1.call-done
  154.7 4.7 %fusion = bf16[3,32,1024]{2,1,0:T(8,128)(2,1)} fusion(bf16[3,1024,1024]{2,1,0:T(8,128)(2,1)} %all-gather.4.cloned.1.call-done, bf16[3,96,1024]{2,1,0:T(8,128)(2,1)S(1)} %reshape.72, pred[3]{0:T(512)(128)(4,1)S(1)} %compare_reduce_fusion), kind=kOutput, calls=%fused_computation.2 | convolution fusion | flops 201523200 | bytes 6685184 | tf_op jit(solution)/shard_map/srn,snb->srb/dot_general | solution.py:90
  (18 shorter events, 0.2 us)
Async XLA Ops:
  7.2 62.3 %all-gather.6.cloned.1.call-start = ((), (), s32[]{:S(2)}) async-start(), calls=%async_computation.8 | async-start | bytes 3342336 | tf_op jit(solution)/shard_map/all_gather | solution.py:55
  7.9 146.8 %all-gather.4.cloned.1.call-start = ((), (), s32[]{:S(2)}) async-start(), calls=%async_computation.7 | async-start | bytes 6488064 | tf_op jit(solution)/shard_map/all_gather | solution.py:60
  33.3 31.1 %copy-start.4 = (s32[16]{0:T(128)S(1)}, s32[16]{0:T(128)}, u32[]{:S(2)}) copy-start(s32[16]{0:T(128)} %param.8) | copy-start | bytes 196
  33.3 33.0 %copy-start.3 = (s32[16]{0:T(128)S(1)}, s32[16]{0:T(128)}, u32[]{:S(2)}) copy-start(s32[16]{0:T(128)} %param.9) | copy-start | bytes 196
  60.8 17.2 %all-to-all-start.2 = ((bf16[8,32,1024]{2,1,0:T(8,128)(2,1)}), bf16[8,32,1024]{2,1,0:T(8,128)(2,1)S(1)}, u32[]{:S(2)}, u32[]{:S(2)}) async-start(bf16[8,32,1024]{2,1,0:T(8,128)(2,1)} %broadcast_in_dim.54), calls=%async_computation.2 | async-start | bytes 1048576 | tf_op jit(solution)/shard_map/all_to_all | solution.py:16
  78.0 9.7 %all-to-all-start.3 = ((bf16[4,32,1280]{2,1,0:T(8,128)(2,1)}), bf16[4,32,1280]{2,1,0:T(8,128)(2,1)S(1)}, u32[]{:S(2)}, u32[]{:S(2)}) async-start(bf16[4,32,1280]{2,1,0:T(8,128)(2,1)} %pad_maximum_fusion.1), calls=%async_computation.3 | async-start | bytes 655360 | tf_op jit(solution)/shard_map/all_to_all | solution.py:16
  99.0 54.0 %copy-start.1 = (f32[3,32,1024]{2,1,0:T(8,128)S(1)}, f32[3,32,1024]{2,1,0:T(8,128)}, u32[]{:S(2)}) copy-start(f32[3,32,1024]{2,1,0:T(8,128)} %param.11) | copy-start | bytes 1179652
  99.0 54.0 %copy-start.2 = (f32[3,32,1024]{2,1,0:T(8,128)S(1)}, f32[3,32,1024]{2,1,0:T(8,128)}, u32[]{:S(2)}) copy-start(f32[3,32,1024]{2,1,0:T(8,128)} %param.10) | copy-start | bytes 1179652
  99.8 28.5 %all-to-all-start.5 = ((bf16[16,48,128]{2,1,0:T(8,128)(2,1)}), bf16[16,48,128]{2,1,0:T(8,128)(2,1)S(1)}, u32[]{:S(2)}, u32[]{:S(2)}) async-start(bf16[16,48,128]{2,1,0:T(8,128)(2,1)} %bitcast.16), calls=%async_computation.5 | async-start | bytes 393216 | tf_op jit(solution)/shard_map/all_to_all | solution.py:16
  128.3 0.7 copy-start
  130.8 21.8 %all-to-all-start.6 = ((bf16[16,3,48,128]{3,2,1,0:T(8,128)(2,1)}), bf16[16,3,48,128]{3,2,1,0:T(8,128)(2,1)S(1)}, u32[]{:S(2)}, u32[]{:S(2)}) async-start(bf16[16,3,48,128]{3,2,1,0:T(8,128)(2,1)} %bitcast.43), calls=%async_computation.6 | async-start | bytes 1179648 | tf_op jit(solution)/shard_map/all_to_all | solution.py:16
Sparse Core Ops, SparseCore 0:
  10.1 50.3 all-gather.5
  63.7 90.9 all-gather.3

commit v3 on v2

--- a/solution.py
+++ b/solution.py
@@ -8,6 +8,8 @@
 from jax.sharding import PartitionSpec as P
 
 NX, NY, NZ, NC = 4, 8, 8, 2
+NL = 2
+NS = 2
 MP = NZ * NC
 F32, BF16 = jnp.float32, jnp.bfloat16
 
@@ -44,24 +46,32 @@
 def body(grad_parts, owner, slot, left_stat, right_stat, left_root, right_root):
     slots, rows, b = left_stat.shape
     ix_panel = b // NX
-    here = lax.axis_index("z") * NC + lax.axis_index("c")
-    iy = lax.axis_index("y")
+    here = lax.axis_index(("zh", "zl", "c"))
+    iy = lax.axis_index("yh") * NL + lax.axis_index("yl")
 
     target = owner * slots + slot
     named = target[None, :] == jnp.arange(MP * slots, dtype=jnp.int32)[:, None]
     block_of = jnp.sum(jnp.where(named, jnp.arange(MP, dtype=jnp.int32)[None, :], 0), axis=1)
     filled = jnp.any(target[None, :] == (here * slots + jnp.arange(slots, dtype=jnp.int32))[:, None], axis=1)
 
-    left_all = lax.all_gather(left_root, ("z", "c"), axis=0)
-    root = lax.dynamic_slice(left_all, (owner[here], slot[here], 0, 0), (1, 1, rows, b)).reshape(rows, NX, ix_panel)
+    roots = lax.all_gather(left_root, ("zh", "c"), axis=0)
 
-    part = add_up(swap(grad_parts[0].reshape(NX, ix_panel, b), "x"))
+    part = add_up(swap(grad_parts[0].reshape(NX * NL, ix_panel // NL, b), ("x", "yl")))
     right_root, part = lax.optimization_barrier((right_root, part))
-    right_full = lax.all_gather(right_root, ("x", "y"), axis=1, tiled=True)
-    chunk = add_up(swap(part.reshape(NY, rows, b), "y"))
+    right_full = lax.all_gather(right_root, ("x", "yh", "yl"), axis=1, tiled=True)
+    chunk = add_up(swap(part.reshape(NY // NL, rows, b), "yh"))
 
-    panel = share(chunk, "y", NY).reshape(ix_panel, b)
-    cross = jnp.broadcast_to(chunk[None], (NX, rows, b))
+    panel = share(chunk, ("yl", "yh"), NY).reshape(ix_panel, b)
+
+    def held(block):
+        place = (owner[block] // (NS * NC)) * NC + owner[block] % NC
+        return lax.dynamic_slice(roots, (place, slot[block], 0, 0), (1, 1, rows, b)).reshape(rows, b)
+
+    root = lax.ppermute(held(here ^ NC), "zl", [(i, i ^ 1) for i in range(NS)])
+    root = jnp.where(((owner[here] ^ here) & NC) == 0, held(here), root).reshape(rows, NX, ix_panel)
+    panel, root = lax.optimization_barrier((panel, root))
+
+    cross = jnp.broadcast_to(lax.dynamic_slice_in_dim(panel, iy * rows, rows, 0)[None], (NX, rows, b))
     cross = swap(jnp.concatenate([cross, root.transpose(1, 0, 2)], axis=2), "x")
     cross, root = cross[:, :, :b].reshape(NX * rows, b), cross[:, :, b:]
 
@@ -79,8 +89,8 @@
     cut_rows, cut_cols = 3 * rows // NC, b // NZ
     items = jnp.concatenate([both, gl], axis=0)
     items = items.reshape(NC, cut_rows, NZ, cut_cols).transpose(2, 0, 1, 3).reshape(MP, cut_rows, cut_cols)
-    items = pick(block_of, swap(items, ("z", "c")))
-    items = swap(items.reshape(MP, slots, cut_rows, cut_cols), ("z", "c"))
+    items = pick(block_of, swap(items, ("zh", "zl", "c")))
+    items = swap(items.reshape(MP, slots, cut_rows, cut_cols), ("zh", "zl", "c"))
     items = items.reshape(NZ, NC, slots, cut_rows, cut_cols).transpose(2, 1, 3, 0, 4).reshape(slots, 3 * rows, b)
     gr, mx, gl = items[:, :rows], items[:, rows : 2 * rows], items[:, 2 * rows :]
 
@@ -93,8 +103,8 @@
 
 
 def solution(mesh):
-    grid = Mesh(np.asarray(mesh.devices).reshape(NX, NY, NZ, NC), ("x", "y", "z", "c"))
-    dp, mp = ("x", "y"), ("z", "c")
+    grid = Mesh(np.asarray(mesh.devices).reshape(NX, NY // NL, NL, NZ // NS, NS, NC), ("x", "yh", "yl", "zh", "zl", "c"))
+    dp, mp = ("x", "yh", "yl"), ("zh", "zl", "c")
     state = P(mp, dp, None)
     return jax.shard_map(
         body,

time: 167 us -> 164 us (0.982)
  blocking collectives: 61.2 us -> 27.4 us
  waiting for transfers between devices: 41.6 us -> 58.4 us
  starting transfers between devices: 28.6 us -> 36.9 us
  between operations: 18.2 us -> 24.3 us
    all_to_all x3 -> x2, blocking collectives: 61.2 us -> 27.4 us  [swap(): return lax.all_to_all(value, axis, 0, 0, tiled=True)]
    all_to_all x4 -> x5, waiting for transfers between devices: 40.3 us -> 55.2 us  [swap(): return lax.all_to_all(value, axis, 0, 0, tiled=True)]
    all_to_all x4 -> x5, starting transfers between devices: 28.6 us -> 32.8 us  [swap(): return lax.all_to_all(value, axis, 0, 0, tiled=True)]
    ppermute x0 -> x1, starting transfers between devices: none -> 3.99 us  [body(): root = lax.ppermute(held(here ^ NC), 'zl', [(i, i ^ 1) for i in range(NS)])]
    all_gather x2, waiting for transfers between devices: 0.57 us -> 2.52 us  [the longest x1 2.5 us: body(): lax.all_gather(right_root, ('x', 'yh', 'yl'), axis=1, tiled=True)]
  transfers between devices with their start and end apart: 6 -> 8, of which waited for: 5 -> 5; matrix products, arithmetic and copies ran while one was open for 6% -> 5% of each run, Pallas kernels for 1% -> 1%
where the time goes in v3:
time: 164 us; the launch traced here: 163 us
  waiting for transfers between devices  58.4 us (36%)
  starting transfers between devices  36.9 us (22%)
  blocking collectives  27.4 us (17%)
  between operations  24.3 us (15%)
  matrix products  5.27 us (3%)
  local copies, waits for them, and re-layouts  4.8 us (3%)
  other arithmetic  4.02 us (2%)
  Pallas kernels  1.8 us (1%)
    all_to_all x5, waiting for transfers between devices, swap(): return lax.all_to_all(value, axis, 0, 0, tiled=True)  55.2 us
    all_to_all x5, starting transfers between devices, swap(): return lax.all_to_all(value, axis, 0, 0, tiled=True)  32.8 us
    all_to_all x2, blocking collectives, swap(): return lax.all_to_all(value, axis, 0, 0, tiled=True)  27.4 us
    dot_general x1, matrix products, body(): jnp.einsum('srn,snb->srb', mx, right_full, preferred_element_type=F32)  4.65 us
    ppermute x1, starting transfers between devices, body(): root = lax.ppermute(held(here ^ NC), 'zl', [(i, i ^ 1) for i in range(NS)])  3.99 us
  transfers between devices with their start and end apart: 8, of which 5 were waited for; matrix products, arithmetic and copies ran while one was open for 5% of the time, Pallas kernels for 1%

profile of v3, /device:TPU:1, one launch (start us, length us, event | category | flops | bytes accessed | tf_op | source)
XLA Modules:
  0.0 162.8 jit_solution(14131703552536928)
XLA Ops:
  7.2 5.9 %all-to-all-start = ((bf16[8,128,1024]{2,1,0:T(8,128)(2,1)}), bf16[8,128,1024]{2,1,0:T(8,128)(2,1)S(1)}, u32[]{:S(2)}, u32[]{:S(2)}) async-start(bf16[8,128,1024]{2,1,0:T(8,128)(2,1)} %bitcast.52), calls=%async_computation | async-start | bytes 4194304 | tf_op jit(solution)/shard_map/all_to_all | solution.py:18
  13.0 0.0 all-gather.6.cloned.1.call-start
  13.1 0.7 all-gather.6.cloned.1.call-update
  13.8 0.0 copy-start.3
  13.8 0.0 copy-start.4
  13.8 0.0 all-gather.4.cloned.1.call-start
  13.8 21.7 %all-to-all-done = bf16[8,128,1024]{2,1,0:T(8,128)(2,1)S(1)} async-done(((bf16[8,128,1024]{2,1,0:T(8,128)(2,1)}), bf16[8,128,1024]{2,1,0:T(8,128)(2,1)S(1)}, u32[]{:S(2)}, u32[]{:S(2)}) %all-to-all-start) | async-done | bytes 2097184 | tf_op jit(solution)/shard_map/all_to_all | solution.py:18
  35.5 0.4 reduce_sum.46
  35.9 0.0 all-gather.4.cloned.1.call-update
  35.9 17.7 %all_to_all.35 = bf16[4,32,1024]{2,1,0:T(8,128)(2,1)S(1)} all-to-all(bf16[4,32,1024]{2,1,0:T(8,128)(2,1)S(1)} %bitcast.54), channel_id=1, replica_groups=mesh['x'=4,'yh'=4,'yl'=2,'zh'=4,'zl'=2,'c'=2] {'yh'}, dimensions={0} | all-to-all | bytes 524288 | tf_op jit(solution)/shard_map/all_to_all | solution.py:18
  53.7 0.9 broadcast_in_dim.54
  54.6 3.5 %all-to-all-start.2 = ((bf16[8,32,1024]{2,1,0:T(8,128)(2,1)}), bf16[8,32,1024]{2,1,0:T(8,128)(2,1)S(1)}, u32[]{:S(2)}, u32[]{:S(2)}) async-start(bf16[8,32,1024]{2,1,0:T(8,128)(2,1)} %broadcast_in_dim.54), calls=%async_computation.2 | async-start | bytes 1048576 | tf_op jit(solution)/shard_map/all_to_all | solution.py:18
  58.1 0.0 copy-done.3
  58.1 0.0 copy-done.4
  58.1 0.7 fusion.2
  63.4 0.0 all-gather.6.cloned.1.call-done
  63.4 0.9 dynamic-slice_bitcast_fusion.1
  64.2 4.0 %collective-permute-start = (bf16[32,1024]{1,0:T(8,128)(2,1)S(1)}, bf16[32,1024]{1,0:T(8,128)(2,1)S(1)}, u32[]{:S(2)}, u32[]{:S(2)}) collective-permute-start(bf16[32,1024]{1,0:T(8,128)(2,1)S(1)} %dynamic-slice_bitcast_fusion.1), channel_id=1, source_target_pairs={{0,2},{2,0},{1,3},{3,1},{4,6},{6,4},{5,7},{7,5},{8,10},{10,8},{9,1... | collective-permute-start | bytes 196616 | tf_op jit(solution)/shard_map/ppermute | solution.py:70
  73.6 0.0 collective-permute-done
  73.6 0.9 bitcast_select_fusion
  74.5 0.0 all-to-all-done.2
  74.6 0.7 pad_maximum_fusion.1
  75.3 4.1 %all-to-all-start.3 = ((bf16[4,32,1280]{2,1,0:T(8,128)(2,1)}), bf16[4,32,1280]{2,1,0:T(8,128)(2,1)S(1)}, u32[]{:S(2)}, u32[]{:S(2)}) async-start(bf16[4,32,1280]{2,1,0:T(8,128)(2,1)} %pad_maximum_fusion.1), calls=%async_computation.3 | async-start | bytes 655360 | tf_op jit(solution)/shard_map/all_to_all | solution.py:18
  79.4 0.2 copy.30
  79.7 5.7 %all-to-all-done.3 = bf16[4,32,1280]{2,1,0:T(8,128)(2,1)S(1)} async-done(((bf16[4,32,1280]{2,1,0:T(8,128)(2,1)}), bf16[4,32,1280]{2,1,0:T(8,128)(2,1)S(1)}, u32[]{:S(2)}, u32[]{:S(2)}) %all-to-all-start.3) | async-done | bytes 327712 | tf_op jit(solution)/shard_map/all_to_all | solution.py:18
  85.4 0.3 convolution_convert_fusion.1
  85.8 0.3 convolution_convert_fusion
  86.1 0.1 pad_maximum_fusion
  86.1 9.7 %all_to_all.36 = bf16[4,64,1152]{2,1,0:T(8,128)(2,1)S(1)} all-to-all(bf16[4,64,1152]{2,1,0:T(8,128)(2,1)S(1)} %pad_maximum_fusion), channel_id=1, replica_groups=mesh['x'=4,'yh'=4,'yl'=2,'zh'=4,'zl'=2,'c'=2] {'x'}, dimensions={0} | all-to-all | bytes 1179648 | tf_op jit(solution)/shard_map/all_to_all | solution.py:18
  95.8 0.1 copy.33
  95.9 0.1 slice_reduce_fusion
  96.1 0.7 copy.34
  96.8 15.9 %all-to-all-start.5 = ((bf16[16,48,128]{2,1,0:T(8,128)(2,1)}), bf16[16,48,128]{2,1,0:T(8,128)(2,1)S(1)}, u32[]{:S(2)}, u32[]{:S(2)}) async-start(bf16[16,48,128]{2,1,0:T(8,128)(2,1)} %bitcast.21), calls=%async_computation.5 | async-start | bytes 393216 | tf_op jit(solution)/shard_map/all_to_all | solution.py:18
  112.7 0.6 select_reduce_fusion.index_ref
  113.3 0.0 copy-start.1
  113.3 9.7 %all-to-all-done.5.in_ref = bf16[16,48,128]{2,1,0:T(8,128)(2,1)S(1)} async-done(((bf16[16,48,128]{2,1,0:T(8,128)(2,1)}), bf16[16,48,128]{2,1,0:T(8,128)(2,1)S(1)}, u32[]{:S(2)}, u32[]{:S(2)}) %all-to-all-start.5) | async-done | bytes 196640 | tf_op jit(solution)/shard_map/all_to_all | solution.py:18
  123.0 0.7 copy-done
  123.7 1.8 %shard_map.94 = bf16[48,48,128]{2,1,0:T(8,128)(2,1)} custom-call(s32[48]{0:T(128)} %select_reduce_fusion.index_ref, bf16[16,48,128]{2,1,0:T(8,128)(2,1)} %copy-done), custom_call_target="tpu_custom_call" | custom-call | tf_op jit(solution)/shard_map/pallas_call | solution.py:35
  125.5 3.5 %all-to-all-start.6 = ((bf16[16,3,48,128]{3,2,1,0:T(8,128)(2,1)}), bf16[16,3,48,128]{3,2,1,0:T(8,128)(2,1)S(1)}, u32[]{:S(2)}, u32[]{:S(2)}) async-start(bf16[16,3,48,128]{3,2,1,0:T(8,128)(2,1)} %bitcast.50), calls=%async_computation.6 | async-start | bytes 1179648 | tf_op jit(solution)/shard_map/all_to_all | solution.py:18
  129.0 0.2 compare_reduce_fusion
  129.2 18.1 %all-to-all-done.6 = bf16[16,3,48,128]{3,2,1,0:T(8,128)(2,1)S(1)} async-done(((bf16[16,3,48,128]{3,2,1,0:T(8,128)(2,1)}), bf16[16,3,48,128]{3,2,1,0:T(8,128)(2,1)S(1)}, u32[]{:S(2)}, u32[]{:S(2)}) %all-to-all-start.6) | async-done | bytes 589856 | tf_op jit(solution)/shard_map/all_to_all | solution.py:18
  147.2 0.2 copy.38
  147.5 0.3 reshape.85
  147.7 0.0 copy-done.1
  147.8 0.0 copy-done.2
  147.8 1.1 add_select_fusion
  148.8 2.5 %all-gather.4.cloned.1.call-done = bf16[3,1024,1024]{2,1,0:T(8,128)(2,1)} async-done(((bf16[3,32,1024]{2,1,0:T(8,128)(2,1)}), bf16[3,1024,1024]{2,1,0:T(8,128)(2,1)}) %all-gather.4.cloned.1.call-update) | async-done | bytes 6291472 | tf_op jit(solution)/shard_map/all_gather | solution.py:61
  151.3 4.7 %fusion = bf16[3,32,1024]{2,1,0:T(8,128)(2,1)} fusion(bf16[3,1024,1024]{2,1,0:T(8,128)(2,1)} %all-gather.4.cloned.1.call-done, bf16[3,96,1024]{2,1,0:T(8,128)(2,1)S(1)} %reshape.85, pred[3]{0:T(512)(128)(4,1)S(1)} %compare_reduce_fusion), kind=kOutput, calls=%fused_computation.2 | convolution fusion | flops 201523200 | bytes 6685184 | tf_op jit(solution)/shard_map/srn,snb->srb/dot_general | solution.py:100
  (20 shorter events, 0.3 us)
Async XLA Ops:
  7.2 28.4 %all-to-all-start = ((bf16[8,128,1024]{2,1,0:T(8,128)(2,1)}), bf16[8,128,1024]{2,1,0:T(8,128)(2,1)S(1)}, u32[]{:S(2)}, u32[]{:S(2)}) async-start(bf16[8,128,1024]{2,1,0:T(8,128)(2,1)} %bitcast.52), calls=%async_computation | async-start | bytes 4194304 | tf_op jit(solution)/shard_map/all_to_all | solution.py:18
  13.0 50.3 %all-gather.6.cloned.1.call-start = ((), (), s32[]{:S(2)}) async-start(), calls=%async_computation.8 | async-start | bytes 1769472 | tf_op jit(solution)/shard_map/all_gather | solution.py:57
  13.8 44.3 %copy-start.3 = (s32[16]{0:T(128)S(1)}, s32[16]{0:T(128)}, u32[]{:S(2)}) copy-start(s32[16]{0:T(128)} %param.9) | copy-start | bytes 196
  13.8 44.3 %copy-start.4 = (s32[16]{0:T(128)S(1)}, s32[16]{0:T(128)}, u32[]{:S(2)}) copy-start(s32[16]{0:T(128)} %param.8) | copy-start | bytes 196
  13.8 137.5 %all-gather.4.cloned.1.call-start = ((), (), s32[]{:S(2)}) async-start(), calls=%async_computation.7 | async-start | bytes 6488064 | tf_op jit(solution)/shard_map/all_gather | solution.py:61
  54.6 19.9 %all-to-all-start.2 = ((bf16[8,32,1024]{2,1,0:T(8,128)(2,1)}), bf16[8,32,1024]{2,1,0:T(8,128)(2,1)S(1)}, u32[]{:S(2)}, u32[]{:S(2)}) async-start(bf16[8,32,1024]{2,1,0:T(8,128)(2,1)} %broadcast_in_dim.54), calls=%async_computation.2 | async-start | bytes 1048576 | tf_op jit(solution)/shard_map/all_to_all | solution.py:18
  64.2 9.4 %collective-permute-start = (bf16[32,1024]{1,0:T(8,128)(2,1)S(1)}, bf16[32,1024]{1,0:T(8,128)(2,1)S(1)}, u32[]{:S(2)}, u32[]{:S(2)}) collective-permute-start(bf16[32,1024]{1,0:T(8,128)(2,1)S(1)} %dynamic-slice_bitcast_fusion.1), channel_id=1, source_target_pairs={{0,2},{2,0},{1,3},{3,1},{4,6},{6,4},{5,7},{7,5},{8,10},{10,8},{9,1... | collective-permute-start | bytes 196616 | tf_op jit(solution)/shard_map/ppermute | solution.py:70
  75.3 10.0 %all-to-all-start.3 = ((bf16[4,32,1280]{2,1,0:T(8,128)(2,1)}), bf16[4,32,1280]{2,1,0:T(8,128)(2,1)S(1)}, u32[]{:S(2)}, u32[]{:S(2)}) async-start(bf16[4,32,1280]{2,1,0:T(8,128)(2,1)} %pad_maximum_fusion.1), calls=%async_computation.3 | async-start | bytes 655360 | tf_op jit(solution)/shard_map/all_to_all | solution.py:18
  96.8 26.2 %all-to-all-start.5 = ((bf16[16,48,128]{2,1,0:T(8,128)(2,1)}), bf16[16,48,128]{2,1,0:T(8,128)(2,1)S(1)}, u32[]{:S(2)}, u32[]{:S(2)}) async-start(bf16[16,48,128]{2,1,0:T(8,128)(2,1)} %bitcast.21), calls=%async_computation.5 | async-start | bytes 393216 | tf_op jit(solution)/shard_map/all_to_all | solution.py:18
  113.3 34.5 %copy-start.1 = (f32[3,32,1024]{2,1,0:T(8,128)S(1)}, f32[3,32,1024]{2,1,0:T(8,128)}, u32[]{:S(2)}) copy-start(f32[3,32,1024]{2,1,0:T(8,128)} %param.11) | copy-start | bytes 1179652
  113.3 34.5 %copy-start.2 = (f32[3,32,1024]{2,1,0:T(8,128)S(1)}, f32[3,32,1024]{2,1,0:T(8,128)}, u32[]{:S(2)}) copy-start(f32[3,32,1024]{2,1,0:T(8,128)} %param.10) | copy-start | bytes 1179652
  123.0 0.7 copy-start
  125.5 21.8 %all-to-all-start.6 = ((bf16[16,3,48,128]{3,2,1,0:T(8,128)(2,1)}), bf16[16,3,48,128]{3,2,1,0:T(8,128)(2,1)S(1)}, u32[]{:S(2)}, u32[]{:S(2)}) async-start(bf16[16,3,48,128]{3,2,1,0:T(8,128)(2,1)} %bitcast.50), calls=%async_computation.6 | async-start | bytes 1179648 | tf_op jit(solution)/shard_map/all_to_all | solution.py:18
Sparse Core Ops, SparseCore 0:
  16.0 40.5 all-gather.5
  59.7 91.5 all-gather.3

commit v4 on v3

--- a/solution.py
+++ b/solution.py
@@ -32,6 +32,7 @@
 
 
 def pick(index, value):
+    value = pltpu.with_memory_space_constraint(value, pltpu.VMEM)
     return pl.pallas_call(
         pick_kernel,
         out_shape=jax.ShapeDtypeStruct(index.shape + value.shape[1:], value.dtype),
@@ -67,9 +68,10 @@
         place = (owner[block] // (NS * NC)) * NC + owner[block] % NC
         return lax.dynamic_slice(roots, (place, slot[block], 0, 0), (1, 1, rows, b)).reshape(rows, b)
 
+    own = held(here)
     root = lax.ppermute(held(here ^ NC), "zl", [(i, i ^ 1) for i in range(NS)])
-    root = jnp.where(((owner[here] ^ here) & NC) == 0, held(here), root).reshape(rows, NX, ix_panel)
-    panel, root = lax.optimization_barrier((panel, root))
+    panel, own, root = lax.optimization_barrier((panel, own, root))
+    root = jnp.where(((owner[here] ^ here) & NC) == 0, own, root).reshape(rows, NX, ix_panel)
 
     cross = jnp.broadcast_to(lax.dynamic_slice_in_dim(panel, iy * rows, rows, 0)[None], (NX, rows, b))
     cross = swap(jnp.concatenate([cross, root.transpose(1, 0, 2)], axis=2), "x")

time: 164 us -> 164 us (level)
  transfers between devices with their start and end apart: 8 -> 8, of which waited for: 5 -> 6; matrix products, arithmetic and copies ran while one was open for 5% -> 5% of each run, Pallas kernels for 1% -> 1%
where the time goes in v4:
time: 164 us; the launch traced here: 163 us
  waiting for transfers between devices  59.3 us (36%)
  starting transfers between devices  37.7 us (23%)
  blocking collectives  27.4 us (17%)
  between operations  24.2 us (15%)
  matrix products  5.27 us (3%)
  local copies, waits for them, and re-layouts  4.16 us (3%)
  other arithmetic  3.17 us (2%)
    all_to_all x5, waiting for transfers between devices, swap(): return lax.all_to_all(value, axis, 0, 0, tiled=True)  55.3 us
    all_to_all x5, starting transfers between devices, swap(): return lax.all_to_all(value, axis, 0, 0, tiled=True)  33.6 us
    all_to_all x2, blocking collectives, swap(): return lax.all_to_all(value, axis, 0, 0, tiled=True)  27.4 us
    dot_general x1, matrix products, body(): jnp.einsum('srn,snb->srb', mx, right_full, preferred_element_type=F32)  4.65 us
    ppermute x1, starting transfers between devices, body(): root = lax.ppermute(held(here ^ NC), 'zl', [(i, i ^ 1) for i in range(NS)])  4 us
  transfers between devices with their start and end apart: 8, of which 6 were waited for; matrix products, arithmetic and copies ran while one was open for 5% of the time, Pallas kernels for 1%

profile of v4, /device:TPU:1, one launch (start us, length us, event | category | flops | bytes accessed | tf_op | source)
XLA Modules:
  0.0 162.8 jit_solution(11178746180339062112)
XLA Ops:
  7.2 5.9 %all-to-all-start = ((bf16[8,128,1024]{2,1,0:T(8,128)(2,1)}), bf16[8,128,1024]{2,1,0:T(8,128)(2,1)S(1)}, u32[]{:S(2)}, u32[]{:S(2)}) async-start(bf16[8,128,1024]{2,1,0:T(8,128)(2,1)} %bitcast.52), calls=%async_computation | async-start | bytes 4194304 | tf_op jit(solution)/shard_map/all_to_all | solution.py:18
  13.0 0.0 all-gather.6.cloned.1.call-start
  13.1 0.7 all-gather.6.cloned.1.call-update
  13.8 0.0 copy-start.2
  13.8 0.0 copy-start.3
  13.8 0.0 all-gather.4.cloned.1.call-start
  13.8 21.7 %all-to-all-done = bf16[8,128,1024]{2,1,0:T(8,128)(2,1)S(1)} async-done(((bf16[8,128,1024]{2,1,0:T(8,128)(2,1)}), bf16[8,128,1024]{2,1,0:T(8,128)(2,1)S(1)}, u32[]{:S(2)}, u32[]{:S(2)}) %all-to-all-start) | async-done | bytes 2097184 | tf_op jit(solution)/shard_map/all_to_all | solution.py:18
  35.5 0.4 reduce_sum.46
  35.9 0.0 all-gather.4.cloned.1.call-update
  35.9 17.7 %all_to_all.35 = bf16[4,32,1024]{2,1,0:T(8,128)(2,1)S(1)} all-to-all(bf16[4,32,1024]{2,1,0:T(8,128)(2,1)S(1)} %bitcast.54), channel_id=1, replica_groups=mesh['x'=4,'yh'=4,'yl'=2,'zh'=4,'zl'=2,'c'=2] {'yh'}, dimensions={0} | all-to-all | bytes 524288 | tf_op jit(solution)/shard_map/all_to_all | solution.py:18
  53.7 0.9 broadcast_in_dim.54
  54.6 3.5 %all-to-all-start.2 = ((bf16[8,32,1024]{2,1,0:T(8,128)(2,1)}), bf16[8,32,1024]{2,1,0:T(8,128)(2,1)S(1)}, u32[]{:S(2)}, u32[]{:S(2)}) async-start(bf16[8,32,1024]{2,1,0:T(8,128)(2,1)} %broadcast_in_dim.54), calls=%async_computation.2 | async-start | bytes 1048576 | tf_op jit(solution)/shard_map/all_to_all | solution.py:18
  58.1 0.0 copy-done.2
  58.1 0.0 copy-done.3
  58.1 0.7 fusion.2
  68.0 0.0 all-gather.6.cloned.1.call-done
  68.1 0.9 dynamic-slice_bitcast_fusion.1
  69.0 4.0 %collective-permute-start = (bf16[32,1024]{1,0:T(8,128)(2,1)S(1)}, bf16[32,1024]{1,0:T(8,128)(2,1)S(1)}, u32[]{:S(2)}, u32[]{:S(2)}) collective-permute-start(bf16[32,1024]{1,0:T(8,128)(2,1)S(1)} %get-tuple-element.13), channel_id=1, source_target_pairs={{0,2},{2,0},{1,3},{3,1},{4,6},{6,4},{5,7},{7,5},{8,10},{10,8},{9,1... | collective-permute-start | bytes 196616 | tf_op jit(solution)/shard_map/ppermute | solution.py:72
  73.6 1.0 collective-permute-done
  74.6 0.0 all-to-all-done.2
  74.7 0.7 pad_maximum_fusion.1
  75.5 4.1 %all-to-all-start.3 = ((bf16[4,32,1280]{2,1,0:T(8,128)(2,1)}), bf16[4,32,1280]{2,1,0:T(8,128)(2,1)S(1)}, u32[]{:S(2)}, u32[]{:S(2)}) async-start(bf16[4,32,1280]{2,1,0:T(8,128)(2,1)} %pad_maximum_fusion.1), calls=%async_computation.3 | async-start | bytes 655360 | tf_op jit(solution)/shard_map/all_to_all | solution.py:18
  79.6 0.2 copy.30
  79.8 5.8 %all-to-all-done.3 = bf16[4,32,1280]{2,1,0:T(8,128)(2,1)S(1)} async-done(((bf16[4,32,1280]{2,1,0:T(8,128)(2,1)}), bf16[4,32,1280]{2,1,0:T(8,128)(2,1)S(1)}, u32[]{:S(2)}, u32[]{:S(2)}) %all-to-all-start.3) | async-done | bytes 327712 | tf_op jit(solution)/shard_map/all_to_all | solution.py:18
  85.6 0.3 convolution_convert_fusion.1
  86.0 0.3 convolution_convert_fusion
  86.3 0.1 pad_maximum_fusion
  86.4 9.7 %all_to_all.36 = bf16[4,64,1152]{2,1,0:T(8,128)(2,1)S(1)} all-to-all(bf16[4,64,1152]{2,1,0:T(8,128)(2,1)S(1)} %pad_maximum_fusion), channel_id=1, replica_groups=mesh['x'=4,'yh'=4,'yl'=2,'zh'=4,'zl'=2,'c'=2] {'x'}, dimensions={0} | all-to-all | bytes 1179648 | tf_op jit(solution)/shard_map/all_to_all | solution.py:18
  96.1 0.1 copy.33
  96.2 0.1 slice_reduce_fusion
  96.4 0.7 copy.34
  97.1 16.7 %all-to-all-start.5 = ((bf16[16,48,128]{2,1,0:T(8,128)(2,1)}), bf16[16,48,128]{2,1,0:T(8,128)(2,1)S(1)}, u32[]{:S(2)}, u32[]{:S(2)}) async-start(bf16[16,48,128]{2,1,0:T(8,128)(2,1)} %bitcast.21), calls=%async_computation.5 | async-start | bytes 393216 | tf_op jit(solution)/shard_map/all_to_all | solution.py:18
  113.8 0.6 select_reduce_fusion.index_ref
  114.4 0.0 copy-start
  114.4 0.0 copy-start.1
  114.4 9.7 %all-to-all-done.5.in_ref = bf16[16,48,128]{2,1,0:T(8,128)(2,1)S(1)} async-done(((bf16[16,48,128]{2,1,0:T(8,128)(2,1)}), bf16[16,48,128]{2,1,0:T(8,128)(2,1)S(1)}, u32[]{:S(2)}, u32[]{:S(2)}) %all-to-all-start.5) | async-done | bytes 196640 | tf_op jit(solution)/shard_map/all_to_all | solution.py:18
  124.1 1.5 shard_map.94
  125.6 3.5 %all-to-all-start.6 = ((bf16[16,3,48,128]{3,2,1,0:T(8,128)(2,1)}), bf16[16,3,48,128]{3,2,1,0:T(8,128)(2,1)S(1)}, u32[]{:S(2)}, u32[]{:S(2)}) async-start(bf16[16,3,48,128]{3,2,1,0:T(8,128)(2,1)} %bitcast.50), calls=%async_computation.6 | async-start | bytes 1179648 | tf_op jit(solution)/shard_map/all_to_all | solution.py:18
  129.1 0.2 compare_reduce_fusion
  129.3 18.1 %all-to-all-done.6 = bf16[16,3,48,128]{3,2,1,0:T(8,128)(2,1)S(1)} async-done(((bf16[16,3,48,128]{3,2,1,0:T(8,128)(2,1)}), bf16[16,3,48,128]{3,2,1,0:T(8,128)(2,1)S(1)}, u32[]{:S(2)}, u32[]{:S(2)}) %all-to-all-start.6) | async-done | bytes 589856 | tf_op jit(solution)/shard_map/all_to_all | solution.py:18
  147.4 0.2 copy.38
  147.7 0.3 reshape.85
  147.9 0.0 copy-done
  147.9 0.0 copy-done.1
  147.9 1.1 add_select_fusion
  149.0 2.3 %all-gather.4.cloned.1.call-done = bf16[3,1024,1024]{2,1,0:T(8,128)(2,1)} async-done(((bf16[3,32,1024]{2,1,0:T(8,128)(2,1)}), bf16[3,1024,1024]{2,1,0:T(8,128)(2,1)}) %all-gather.4.cloned.1.call-update) | async-done | bytes 6291472 | tf_op jit(solution)/shard_map/all_gather | solution.py:62
  151.4 4.7 %fusion = bf16[3,32,1024]{2,1,0:T(8,128)(2,1)} fusion(bf16[3,1024,1024]{2,1,0:T(8,128)(2,1)} %all-gather.4.cloned.1.call-done, bf16[3,96,1024]{2,1,0:T(8,128)(2,1)S(1)} %reshape.85, pred[3]{0:T(512)(128)(4,1)S(1)} %compare_reduce_fusion), kind=kOutput, calls=%fused_computation.2 | convolution fusion | flops 201523200 | bytes 6685184 | tf_op jit(solution)/shard_map/srn,snb->srb/dot_general | solution.py:102
  (19 shorter events, 0.3 us)
Async XLA Ops:
  7.2 28.4 %all-to-all-start = ((bf16[8,128,1024]{2,1,0:T(8,128)(2,1)}), bf16[8,128,1024]{2,1,0:T(8,128)(2,1)S(1)}, u32[]{:S(2)}, u32[]{:S(2)}) async-start(bf16[8,128,1024]{2,1,0:T(8,128)(2,1)} %bitcast.52), calls=%async_computation | async-start | bytes 4194304 | tf_op jit(solution)/shard_map/all_to_all | solution.py:18
  13.0 55.0 %all-gather.6.cloned.1.call-start = ((), (), s32[]{:S(2)}) async-start(), calls=%async_computation.8 | async-start | bytes 1769472 | tf_op jit(solution)/shard_map/all_gather | solution.py:58
  13.8 44.3 %copy-start.2 = (s32[16]{0:T(128)S(1)}, s32[16]{0:T(128)}, u32[]{:S(2)}) copy-start(s32[16]{0:T(128)} %param.9) | copy-start | bytes 196
  13.8 44.3 %copy-start.3 = (s32[16]{0:T(128)S(1)}, s32[16]{0:T(128)}, u32[]{:S(2)}) copy-start(s32[16]{0:T(128)} %param.8) | copy-start | bytes 196
  13.8 137.6 %all-gather.4.cloned.1.call-start = ((), (), s32[]{:S(2)}) async-start(), calls=%async_computation.7 | async-start | bytes 6488064 | tf_op jit(solution)/shard_map/all_gather | solution.py:62
  54.6 20.0 %all-to-all-start.2 = ((bf16[8,32,1024]{2,1,0:T(8,128)(2,1)}), bf16[8,32,1024]{2,1,0:T(8,128)(2,1)S(1)}, u32[]{:S(2)}, u32[]{:S(2)}) async-start(bf16[8,32,1024]{2,1,0:T(8,128)(2,1)} %broadcast_in_dim.54), calls=%async_computation.2 | async-start | bytes 1048576 | tf_op jit(solution)/shard_map/all_to_all | solution.py:18
  69.0 5.6 %collective-permute-start = (bf16[32,1024]{1,0:T(8,128)(2,1)S(1)}, bf16[32,1024]{1,0:T(8,128)(2,1)S(1)}, u32[]{:S(2)}, u32[]{:S(2)}) collective-permute-start(bf16[32,1024]{1,0:T(8,128)(2,1)S(1)} %get-tuple-element.13), channel_id=1, source_target_pairs={{0,2},{2,0},{1,3},{3,1},{4,6},{6,4},{5,7},{7,5},{8,10},{10,8},{9,1... | collective-permute-start | bytes 196616 | tf_op jit(solution)/shard_map/ppermute | solution.py:72
  75.5 10.1 %all-to-all-start.3 = ((bf16[4,32,1280]{2,1,0:T(8,128)(2,1)}), bf16[4,32,1280]{2,1,0:T(8,128)(2,1)S(1)}, u32[]{:S(2)}, u32[]{:S(2)}) async-start(bf16[4,32,1280]{2,1,0:T(8,128)(2,1)} %pad_maximum_fusion.1), calls=%async_computation.3 | async-start | bytes 655360 | tf_op jit(solution)/shard_map/all_to_all | solution.py:18
  97.1 27.0 %all-to-all-start.5 = ((bf16[16,48,128]{2,1,0:T(8,128)(2,1)}), bf16[16,48,128]{2,1,0:T(8,128)(2,1)S(1)}, u32[]{:S(2)}, u32[]{:S(2)}) async-start(bf16[16,48,128]{2,1,0:T(8,128)(2,1)} %bitcast.21), calls=%async_computation.5 | async-start | bytes 393216 | tf_op jit(solution)/shard_map/all_to_all | solution.py:18
  114.4 33.5 %copy-start = (f32[3,32,1024]{2,1,0:T(8,128)S(1)}, f32[3,32,1024]{2,1,0:T(8,128)}, u32[]{:S(2)}) copy-start(f32[3,32,1024]{2,1,0:T(8,128)} %param.11) | copy-start | bytes 1179652
  114.4 33.5 %copy-start.1 = (f32[3,32,1024]{2,1,0:T(8,128)S(1)}, f32[3,32,1024]{2,1,0:T(8,128)}, u32[]{:S(2)}) copy-start(f32[3,32,1024]{2,1,0:T(8,128)} %param.10) | copy-start | bytes 1179652
  125.6 21.8 %all-to-all-start.6 = ((bf16[16,3,48,128]{3,2,1,0:T(8,128)(2,1)}), bf16[16,3,48,128]{3,2,1,0:T(8,128)(2,1)S(1)}, u32[]{:S(2)}, u32[]{:S(2)}) async-start(bf16[16,3,48,128]{3,2,1,0:T(8,128)(2,1)} %bitcast.50), calls=%async_computation.6 | async-start | bytes 1179648 | tf_op jit(solution)/shard_map/all_to_all | solution.py:18
Sparse Core Ops, SparseCore 0:
  16.0 40.5 all-gather.5
  59.7 91.5 all-gather.3

commit v5 on v4

--- a/solution.py
+++ b/solution.py
@@ -64,14 +64,21 @@
 
     panel = share(chunk, ("yl", "yh"), NY).reshape(ix_panel, b)
 
-    def held(block):
-        place = (owner[block] // (NS * NC)) * NC + owner[block] % NC
-        return lax.dynamic_slice(roots, (place, slot[block], 0, 0), (1, 1, rows, b)).reshape(rows, b)
+    bands = jnp.arange(MP, dtype=jnp.int32)
+    place = ((owner >> 2) * NC + (owner & 1)) * slots + slot
+    place = place + jnp.where(((owner ^ bands) & NC) == 0, 0, MP * slots)
+    mine = jnp.sum(jnp.where(bands == here, place, 0))
+    other = jnp.sum(jnp.where(bands == here ^ NC, place, 0))
+    roots = roots.reshape(NZ // NS * NC * slots, rows, b)
 
-    own = held(here)
-    root = lax.ppermute(held(here ^ NC), "zl", [(i, i ^ 1) for i in range(NS)])
+    def held(place):
+        place = jnp.where(place < MP * slots, place, place - MP * slots)
+        return lax.dynamic_index_in_dim(roots, place, 0, keepdims=False)
+
+    own = held(mine)
+    root = lax.ppermute(held(other), "zl", [(i, i ^ 1) for i in range(NS)])
     panel, own, root = lax.optimization_barrier((panel, own, root))
-    root = jnp.where(((owner[here] ^ here) & NC) == 0, own, root).reshape(rows, NX, ix_panel)
+    root = jnp.where(mine < MP * slots, own, root).reshape(rows, NX, ix_panel)
 
     cross = jnp.broadcast_to(lax.dynamic_slice_in_dim(panel, iy * rows, rows, 0)[None], (NX, rows, b))
     cross = swap(jnp.concatenate([cross, root.transpose(1, 0, 2)], axis=2), "x")

time: 164 us -> 164 us (level)
  between operations: 24.2 us -> 18.2 us
  waiting for transfers between devices: 59.3 us -> 63.7 us
    all_gather x1, waiting for transfers between devices: 2.34 us -> 5.22 us  [body(): lax.all_gather(right_root, ('x', 'yh', 'yl'), axis=1, tiled=True)]
where the time goes in v5:
time: 164 us; the launch traced here: 163 us
  waiting for transfers between devices  63.7 us (39%)
  starting transfers between devices  39.1 us (24%)
  blocking collectives  27.6 us (17%)
  between operations  18.2 us (11%)
  matrix products  5.27 us (3%)
  other arithmetic  3.83 us (2%)
  local copies, waits for them, and re-layouts  3.48 us (2%)
    all_to_all x5, waiting for transfers between devices, swap(): return lax.all_to_all(value, axis, 0, 0, tiled=True)  55.9 us
    all_to_all x5, starting transfers between devices, swap(): return lax.all_to_all(value, axis, 0, 0, tiled=True)  35.1 us
    all_to_all x2, blocking collectives, swap(): return lax.all_to_all(value, axis, 0, 0, tiled=True)  27.6 us
    all_gather x1, waiting for transfers between devices, body(): lax.all_gather(right_root, ('x', 'yh', 'yl'), axis=1, tiled=True)  5.22 us
    dot_general x1, matrix products, body(): jnp.einsum('srn,snb->srb', mx, right_full, preferred_element_type=F32)  4.65 us
    ppermute x1, starting transfers between devices, body(): root = lax.ppermute(held(other), 'zl', [(i, i ^ 1) for i in range(NS)])  4 us
  transfers between devices with their start and end apart: 8, of which 6 were waited for; matrix products, arithmetic and copies ran while one was open for 5% of the time, Pallas kernels for 1%

profile of v5, /device:TPU:1, one launch (start us, length us, event | category | flops | bytes accessed | tf_op | source)
XLA Modules:
  0.0 162.8 jit_solution(14686550569913467236)
XLA Ops:
  7.2 5.9 %all-to-all-start = ((bf16[8,128,1024]{2,1,0:T(8,128)(2,1)}), bf16[8,128,1024]{2,1,0:T(8,128)(2,1)S(1)}, u32[]{:S(2)}, u32[]{:S(2)}) async-start(bf16[8,128,1024]{2,1,0:T(8,128)(2,1)} %bitcast.47), calls=%async_computation | async-start | bytes 4194304 | tf_op jit(solution)/shard_map/all_to_all | solution.py:18
  13.0 0.0 all-gather.6.cloned.1.call-start
  13.1 0.7 all-gather.6.cloned.1.call-update
  13.8 0.0 copy-start.2
  13.8 0.0 copy-start.3
  13.8 0.0 all-gather.4.cloned.1.call-start
  13.8 21.7 %all-to-all-done = bf16[8,128,1024]{2,1,0:T(8,128)(2,1)S(1)} async-done(((bf16[8,128,1024]{2,1,0:T(8,128)(2,1)}), bf16[8,128,1024]{2,1,0:T(8,128)(2,1)S(1)}, u32[]{:S(2)}, u32[]{:S(2)}) %all-to-all-start) | async-done | bytes 2097184 | tf_op jit(solution)/shard_map/all_to_all | solution.py:18
  35.5 0.4 reduce_sum.64
  35.9 0.0 all-gather.4.cloned.1.call-update
  35.9 17.7 %all_to_all.35 = bf16[4,32,1024]{2,1,0:T(8,128)(2,1)S(1)} all-to-all(bf16[4,32,1024]{2,1,0:T(8,128)(2,1)S(1)} %bitcast.49), channel_id=1, replica_groups=mesh['x'=4,'yh'=4,'yl'=2,'zh'=4,'zl'=2,'c'=2] {'yh'}, dimensions={0} | all-to-all | bytes 524288 | tf_op jit(solution)/shard_map/all_to_all | solution.py:18
  53.7 0.9 broadcast_in_dim.63
  54.6 3.5 %all-to-all-start.2 = ((bf16[8,32,1024]{2,1,0:T(8,128)(2,1)}), bf16[8,32,1024]{2,1,0:T(8,128)(2,1)S(1)}, u32[]{:S(2)}, u32[]{:S(2)}) async-start(bf16[8,32,1024]{2,1,0:T(8,128)(2,1)} %broadcast_in_dim.63), calls=%async_computation.2 | async-start | bytes 1048576 | tf_op jit(solution)/shard_map/all_to_all | solution.py:18
  58.1 0.0 copy-done.2
  58.1 0.0 copy-done.3
  58.1 0.6 fusion.4
  62.7 0.0 all-gather.6.cloned.1.call-done
  62.7 0.9 dynamic-slice_bitcast_fusion.2
  63.6 4.0 %collective-permute-start = (bf16[32,1024]{1,0:T(8,128)(2,1)S(1)}, bf16[32,1024]{1,0:T(8,128)(2,1)S(1)}, u32[]{:S(2)}, u32[]{:S(2)}) collective-permute-start(bf16[32,1024]{1,0:T(8,128)(2,1)S(1)} %get-tuple-element.15), channel_id=1, source_target_pairs={{0,2},{2,0},{1,3},{3,1},{4,6},{6,4},{5,7},{7,5},{8,10},{10,8},{9,1... | collective-permute-start | bytes 196616 | tf_op jit(solution)/shard_map/ppermute | solution.py:79
  67.6 1.9 %collective-permute-done = bf16[32,1024]{1,0:T(8,128)(2,1)S(1)} collective-permute-done((bf16[32,1024]{1,0:T(8,128)(2,1)S(1)}, bf16[32,1024]{1,0:T(8,128)(2,1)S(1)}, u32[]{:S(2)}, u32[]{:S(2)}) %collective-permute-start) | collective-permute-done | bytes 65568 | tf_op jit(solution)/shard_map/ppermute | solution.py:79
  69.5 0.0 all-to-all-done.2
  69.6 0.7 pad_maximum_fusion.1
  70.4 6.6 %all-to-all-start.3 = ((bf16[4,32,1280]{2,1,0:T(8,128)(2,1)}), bf16[4,32,1280]{2,1,0:T(8,128)(2,1)S(1)}, u32[]{:S(2)}, u32[]{:S(2)}) async-start(bf16[4,32,1280]{2,1,0:T(8,128)(2,1)} %pad_maximum_fusion.1), calls=%async_computation.3 | async-start | bytes 655360 | tf_op jit(solution)/shard_map/all_to_all | solution.py:18
  77.0 0.2 copy.30
  77.2 6.4 %all-to-all-done.3 = bf16[4,32,1280]{2,1,0:T(8,128)(2,1)S(1)} async-done(((bf16[4,32,1280]{2,1,0:T(8,128)(2,1)}), bf16[4,32,1280]{2,1,0:T(8,128)(2,1)S(1)}, u32[]{:S(2)}, u32[]{:S(2)}) %all-to-all-start.3) | async-done | bytes 327712 | tf_op jit(solution)/shard_map/all_to_all | solution.py:18
  83.6 0.3 convolution_convert_fusion.1
  84.0 0.3 convolution_convert_fusion
  84.3 0.1 pad_maximum_fusion
  84.4 9.9 %all_to_all.36 = bf16[4,64,1152]{2,1,0:T(8,128)(2,1)S(1)} all-to-all(bf16[4,64,1152]{2,1,0:T(8,128)(2,1)S(1)} %pad_maximum_fusion), channel_id=1, replica_groups=mesh['x'=4,'yh'=4,'yl'=2,'zh'=4,'zl'=2,'c'=2] {'x'}, dimensions={0} | all-to-all | bytes 1179648 | tf_op jit(solution)/shard_map/all_to_all | solution.py:18
  94.3 0.1 copy.33
  94.4 0.1 slice_reduce_fusion
  94.5 0.7 copy.34
  95.2 15.7 %all-to-all-start.5 = ((bf16[16,48,128]{2,1,0:T(8,128)(2,1)}), bf16[16,48,128]{2,1,0:T(8,128)(2,1)S(1)}, u32[]{:S(2)}, u32[]{:S(2)}) async-start(bf16[16,48,128]{2,1,0:T(8,128)(2,1)} %bitcast.16), calls=%async_computation.5 | async-start | bytes 393216 | tf_op jit(solution)/shard_map/all_to_all | solution.py:18
  110.9 0.6 select_reduce_fusion.index_ref
  111.5 0.0 copy-start
  111.5 0.0 copy-start.1
  111.5 9.7 %all-to-all-done.5.in_ref = bf16[16,48,128]{2,1,0:T(8,128)(2,1)S(1)} async-done(((bf16[16,48,128]{2,1,0:T(8,128)(2,1)}), bf16[16,48,128]{2,1,0:T(8,128)(2,1)S(1)}, u32[]{:S(2)}, u32[]{:S(2)}) %all-to-all-start.5) | async-done | bytes 196640 | tf_op jit(solution)/shard_map/all_to_all | solution.py:18
  121.2 1.5 shard_map.94
  122.8 3.5 %all-to-all-start.6 = ((bf16[16,3,48,128]{3,2,1,0:T(8,128)(2,1)}), bf16[16,3,48,128]{3,2,1,0:T(8,128)(2,1)S(1)}, u32[]{:S(2)}, u32[]{:S(2)}) async-start(bf16[16,3,48,128]{3,2,1,0:T(8,128)(2,1)} %bitcast.45), calls=%async_computation.6 | async-start | bytes 1179648 | tf_op jit(solution)/shard_map/all_to_all | solution.py:18
  126.3 0.2 compare_reduce_fusion
  126.5 18.1 %all-to-all-done.6 = bf16[16,3,48,128]{3,2,1,0:T(8,128)(2,1)S(1)} async-done(((bf16[16,3,48,128]{3,2,1,0:T(8,128)(2,1)}), bf16[16,3,48,128]{3,2,1,0:T(8,128)(2,1)S(1)}, u32[]{:S(2)}, u32[]{:S(2)}) %all-to-all-start.6) | async-done | bytes 589856 | tf_op jit(solution)/shard_map/all_to_all | solution.py:18
  144.5 0.2 copy.38
  144.8 0.3 reshape.81
  145.0 0.0 copy-done
  145.0 0.0 copy-done.1
  145.0 1.1 add_select_fusion
  146.1 5.2 %all-gather.4.cloned.1.call-done = bf16[3,1024,1024]{2,1,0:T(8,128)(2,1)} async-done(((bf16[3,32,1024]{2,1,0:T(8,128)(2,1)}), bf16[3,1024,1024]{2,1,0:T(8,128)(2,1)}) %all-gather.4.cloned.1.call-update) | async-done | bytes 6291472 | tf_op jit(solution)/shard_map/all_gather | solution.py:62
  151.3 4.7 %fusion = bf16[3,32,1024]{2,1,0:T(8,128)(2,1)} fusion(bf16[3,1024,1024]{2,1,0:T(8,128)(2,1)} %all-gather.4.cloned.1.call-done, bf16[3,96,1024]{2,1,0:T(8,128)(2,1)S(1)} %reshape.81, pred[3]{0:T(512)(128)(4,1)S(1)} %compare_reduce_fusion), kind=kOutput, calls=%fused_computation.2 | convolution fusion | flops 201523200 | bytes 6685184 | tf_op jit(solution)/shard_map/srn,snb->srb/dot_general | solution.py:109
  (18 shorter events, 0.3 us)
Async XLA Ops:
  7.2 28.4 %all-to-all-start = ((bf16[8,128,1024]{2,1,0:T(8,128)(2,1)}), bf16[8,128,1024]{2,1,0:T(8,128)(2,1)S(1)}, u32[]{:S(2)}, u32[]{:S(2)}) async-start(bf16[8,128,1024]{2,1,0:T(8,128)(2,1)} %bitcast.47), calls=%async_computation | async-start | bytes 4194304 | tf_op jit(solution)/shard_map/all_to_all | solution.py:18
  13.0 49.7 %all-gather.6.cloned.1.call-start = ((), (), s32[]{:S(2)}) async-start(), calls=%async_computation.8 | async-start | bytes 1769472 | tf_op jit(solution)/shard_map/all_gather | solution.py:58
  13.8 44.3 %copy-start.2 = (s32[16]{0:T(128)S(1)}, s32[16]{0:T(128)}, u32[]{:S(2)}) copy-start(s32[16]{0:T(128)} %param.8) | copy-start | bytes 196
  13.8 44.3 %copy-start.3 = (s32[16]{0:T(128)S(1)}, s32[16]{0:T(128)}, u32[]{:S(2)}) copy-start(s32[16]{0:T(128)} %param.9) | copy-start | bytes 196
  13.8 137.5 %all-gather.4.cloned.1.call-start = ((), (), s32[]{:S(2)}) async-start(), calls=%async_computation.7 | async-start | bytes 6488064 | tf_op jit(solution)/shard_map/all_gather | solution.py:62
  54.6 14.9 %all-to-all-start.2 = ((bf16[8,32,1024]{2,1,0:T(8,128)(2,1)}), bf16[8,32,1024]{2,1,0:T(8,128)(2,1)S(1)}, u32[]{:S(2)}, u32[]{:S(2)}) async-start(bf16[8,32,1024]{2,1,0:T(8,128)(2,1)} %broadcast_in_dim.63), calls=%async_computation.2 | async-start | bytes 1048576 | tf_op jit(solution)/shard_map/all_to_all | solution.py:18
  63.6 5.9 %collective-permute-start = (bf16[32,1024]{1,0:T(8,128)(2,1)S(1)}, bf16[32,1024]{1,0:T(8,128)(2,1)S(1)}, u32[]{:S(2)}, u32[]{:S(2)}) collective-permute-start(bf16[32,1024]{1,0:T(8,128)(2,1)S(1)} %get-tuple-element.15), channel_id=1, source_target_pairs={{0,2},{2,0},{1,3},{3,1},{4,6},{6,4},{5,7},{7,5},{8,10},{10,8},{9,1... | collective-permute-start | bytes 196616 | tf_op jit(solution)/shard_map/ppermute | solution.py:79
  70.4 13.2 %all-to-all-start.3 = ((bf16[4,32,1280]{2,1,0:T(8,128)(2,1)}), bf16[4,32,1280]{2,1,0:T(8,128)(2,1)S(1)}, u32[]{:S(2)}, u32[]{:S(2)}) async-start(bf16[4,32,1280]{2,1,0:T(8,128)(2,1)} %pad_maximum_fusion.1), calls=%async_computation.3 | async-start | bytes 655360 | tf_op jit(solution)/shard_map/all_to_all | solution.py:18
  95.2 26.0 %all-to-all-start.5 = ((bf16[16,48,128]{2,1,0:T(8,128)(2,1)}), bf16[16,48,128]{2,1,0:T(8,128)(2,1)S(1)}, u32[]{:S(2)}, u32[]{:S(2)}) async-start(bf16[16,48,128]{2,1,0:T(8,128)(2,1)} %bitcast.16), calls=%async_computation.5 | async-start | bytes 393216 | tf_op jit(solution)/shard_map/all_to_all | solution.py:18
  111.5 33.5 %copy-start = (f32[3,32,1024]{2,1,0:T(8,128)S(1)}, f32[3,32,1024]{2,1,0:T(8,128)}, u32[]{:S(2)}) copy-start(f32[3,32,1024]{2,1,0:T(8,128)} %param.11) | copy-start | bytes 1179652
  111.5 33.5 %copy-start.1 = (f32[3,32,1024]{2,1,0:T(8,128)S(1)}, f32[3,32,1024]{2,1,0:T(8,128)}, u32[]{:S(2)}) copy-start(f32[3,32,1024]{2,1,0:T(8,128)} %param.10) | copy-start | bytes 1179652
  122.8 21.8 %all-to-all-start.6 = ((bf16[16,3,48,128]{3,2,1,0:T(8,128)(2,1)}), bf16[16,3,48,128]{3,2,1,0:T(8,128)(2,1)S(1)}, u32[]{:S(2)}, u32[]{:S(2)}) async-start(bf16[16,3,48,128]{3,2,1,0:T(8,128)(2,1)} %bitcast.45), calls=%async_computation.6 | async-start | bytes 1179648 | tf_op jit(solution)/shard_map/all_to_all | solution.py:18
Sparse Core Ops, SparseCore 0:
  16.0 40.5 all-gather.5
  59.7 91.5 all-gather.3

commit v6 on v5

--- a/solution.py
+++ b/solution.py
@@ -42,6 +42,37 @@
         ],
         out_specs=pl.BlockSpec(memory_space=pltpu.VMEM),
     )(index, value)
+
+
+def multiply_kernel(filled_ref, left_ref, right_ref, out_ref, held, arrived):
+    parts = [(i, j) for i in range(held.shape[0]) for j in range(held.shape[1])]
+    copies = [pltpu.make_async_copy(right_ref.at[i, j], held.at[i, j], arrived.at[i, j]) for i, j in parts]
+    for copy in copies:
+        copy.start()
+    deep = held.shape[2]
+    for i in range(held.shape[0]):
+        total = None
+        for j in range(held.shape[1]):
+            copies[i * held.shape[1] + j].wait()
+            term = jnp.dot(left_ref[i, :, j * deep : (j + 1) * deep], held[i, j], preferred_element_type=F32)
+            total = term if total is None else total + term
+        out_ref[i] = jnp.where(filled_ref[i] > 0, total, 0.0).astype(out_ref.dtype)
+
+
+def multiply(filled, left, right, cuts):
+    slots, rows, b = left.shape
+    vmem = pl.BlockSpec(memory_space=pltpu.VMEM)
+    return pl.pallas_call(
+        multiply_kernel,
+        out_shape=jax.ShapeDtypeStruct(left.shape, left.dtype),
+        in_specs=[pl.BlockSpec(memory_space=pltpu.SMEM), vmem, pl.BlockSpec(memory_space=pl.ANY)],
+        out_specs=vmem,
+        scratch_shapes=[
+            pltpu.VMEM((slots, cuts, b // cuts, b), right.dtype),
+            pltpu.SemaphoreType.DMA((slots, cuts)),
+        ],
+        compiler_params=pltpu.CompilerParams(vmem_limit_bytes=60 << 20),
+    )(filled.astype(jnp.int32), left, right.reshape(slots, cuts, b // cuts, b))
 
 
 def body(grad_parts, owner, slot, left_stat, right_stat, left_root, right_root):
@@ -106,8 +137,7 @@
     keeper = filled[:, None, None]
     new_left = jnp.where(keeper, 0.95 * left_stat + 0.05 * gl.astype(F32), left_stat)
     new_right = jnp.where(keeper, 0.95 * right_stat + 0.05 * gr.astype(F32), right_stat)
-    update = jnp.einsum("srn,snb->srb", mx, right_full, preferred_element_type=F32)
-    update = jnp.where(keeper, update, 0.0).astype(BF16)
+    update = multiply(filled, mx, right_full, 4)
     return new_left, new_right, update
 
 

time: 164 us -> 164 us (level)
  Pallas kernels: 1.55 us -> 6.24 us
  matrix products: 5.27 us -> 0.62 us
    pallas_call x0 -> x1, Pallas kernels: none -> 4.69 us  [multiply(): pl.pallas_call(multiply_kernel, out_shape=jax.ShapeDtypeStruct(left.shape...]
    dot_general x1 -> x0, matrix products: 4.65 us -> none  [body(): jnp.einsum('srn,snb->srb', mx, right_full, preferred_element_type=F32)]
  transfers between devices with their start and end apart: 8 -> 8, of which waited for: 6 -> 6; matrix products, arithmetic and copies ran while one was open for 5% -> 6% of each run, Pallas kernels for 1% -> 1%
where the time goes in v6:
time: 164 us; the launch traced here: 163 us
  waiting for transfers between devices  62.5 us (38%)
  starting transfers between devices  39.1 us (24%)
  blocking collectives  27.6 us (17%)
  between operations  18.2 us (11%)
  Pallas kernels  6.24 us (4%)
  other arithmetic  4.37 us (3%)
  local copies, waits for them, and re-layouts  4.18 us (3%)
    all_to_all x5, waiting for transfers between devices, swap(): return lax.all_to_all(value, axis, 0, 0, tiled=True)  55.4 us
    all_to_all x5, starting transfers between devices, swap(): return lax.all_to_all(value, axis, 0, 0, tiled=True)  35.1 us
    all_to_all x2, blocking collectives, swap(): return lax.all_to_all(value, axis, 0, 0, tiled=True)  27.6 us
    pallas_call x1, Pallas kernels, multiply(): pl.pallas_call(multiply_kernel, out_shape=jax.ShapeDtypeStruct(left.shape...  4.69 us
    all_gather x1, waiting for transfers between devices, body(): lax.all_gather(right_root, ('x', 'yh', 'yl'), axis=1, tiled=True)  4.52 us
    ppermute x1, starting transfers between devices, body(): root = lax.ppermute(held(other), 'zl', [(i, i ^ 1) for i in range(NS)])  4 us
  transfers between devices with their start and end apart: 8, of which 6 were waited for; matrix products, arithmetic and copies ran while one was open for 6% of the time, Pallas kernels for 1%

profile of v6, /device:TPU:1, one launch (start us, length us, event | category | flops | bytes accessed | tf_op | source)
XLA Modules:
  0.0 162.9 jit_solution(3899408244395625916)
XLA Ops:
  7.2 5.9 %all-to-all-start = ((bf16[8,128,1024]{2,1,0:T(8,128)(2,1)}), bf16[8,128,1024]{2,1,0:T(8,128)(2,1)S(1)}, u32[]{:S(2)}, u32[]{:S(2)}) async-start(bf16[8,128,1024]{2,1,0:T(8,128)(2,1)} %bitcast.46), calls=%async_computation | async-start | bytes 4194304 | tf_op jit(solution)/shard_map/all_to_all | solution.py:18
  13.0 0.0 all-gather.6.cloned.1.call-start
  13.1 0.7 all-gather.6.cloned.1.call-update
  13.8 0.0 all-gather.4.cloned.1.call-start
  13.8 21.7 %all-to-all-done = bf16[8,128,1024]{2,1,0:T(8,128)(2,1)S(1)} async-done(((bf16[8,128,1024]{2,1,0:T(8,128)(2,1)}), bf16[8,128,1024]{2,1,0:T(8,128)(2,1)S(1)}, u32[]{:S(2)}, u32[]{:S(2)}) %all-to-all-start) | async-done | bytes 2097184 | tf_op jit(solution)/shard_map/all_to_all | solution.py:18
  35.5 0.4 reduce_sum.64
  35.9 0.0 copy-start.2
  35.9 0.0 copy-start.3
  35.9 0.0 all-gather.4.cloned.1.call-update
  35.9 17.7 %all_to_all.35 = bf16[4,32,1024]{2,1,0:T(8,128)(2,1)S(1)} all-to-all(bf16[4,32,1024]{2,1,0:T(8,128)(2,1)S(1)} %bitcast.48), channel_id=1, replica_groups=mesh['x'=4,'yh'=4,'yl'=2,'zh'=4,'zl'=2,'c'=2] {'yh'}, dimensions={0} | all-to-all | bytes 524288 | tf_op jit(solution)/shard_map/all_to_all | solution.py:18
  53.7 0.9 broadcast_in_dim.53
  54.6 3.5 %all-to-all-start.2 = ((bf16[8,32,1024]{2,1,0:T(8,128)(2,1)}), bf16[8,32,1024]{2,1,0:T(8,128)(2,1)S(1)}, u32[]{:S(2)}, u32[]{:S(2)}) async-start(bf16[8,32,1024]{2,1,0:T(8,128)(2,1)} %broadcast_in_dim.53), calls=%async_computation.2 | async-start | bytes 1048576 | tf_op jit(solution)/shard_map/all_to_all | solution.py:18
  58.1 0.0 copy-done.2
  58.1 0.0 copy-done.3
  58.2 0.6 fusion.2
  62.7 0.0 all-gather.6.cloned.1.call-done
  62.7 0.9 dynamic-slice_bitcast_fusion.2
  63.6 4.0 %collective-permute-start = (bf16[32,1024]{1,0:T(8,128)(2,1)S(1)}, bf16[32,1024]{1,0:T(8,128)(2,1)S(1)}, u32[]{:S(2)}, u32[]{:S(2)}) collective-permute-start(bf16[32,1024]{1,0:T(8,128)(2,1)S(1)} %get-tuple-element.15), channel_id=1, source_target_pairs={{0,2},{2,0},{1,3},{3,1},{4,6},{6,4},{5,7},{7,5},{8,10},{10,8},{9,1... | collective-permute-start | bytes 196616 | tf_op jit(solution)/shard_map/ppermute | solution.py:110
  67.6 1.9 %collective-permute-done = bf16[32,1024]{1,0:T(8,128)(2,1)S(1)} collective-permute-done((bf16[32,1024]{1,0:T(8,128)(2,1)S(1)}, bf16[32,1024]{1,0:T(8,128)(2,1)S(1)}, u32[]{:S(2)}, u32[]{:S(2)}) %collective-permute-start) | collective-permute-done | bytes 65568 | tf_op jit(solution)/shard_map/ppermute | solution.py:110
  69.6 0.0 all-to-all-done.2
  69.7 0.7 pad_maximum_fusion.1
  70.4 6.6 %all-to-all-start.3 = ((bf16[4,32,1280]{2,1,0:T(8,128)(2,1)}), bf16[4,32,1280]{2,1,0:T(8,128)(2,1)S(1)}, u32[]{:S(2)}, u32[]{:S(2)}) async-start(bf16[4,32,1280]{2,1,0:T(8,128)(2,1)} %pad_maximum_fusion.1), calls=%async_computation.3 | async-start | bytes 655360 | tf_op jit(solution)/shard_map/all_to_all | solution.py:18
  77.0 0.2 copy.29
  77.2 6.4 %all-to-all-done.3 = bf16[4,32,1280]{2,1,0:T(8,128)(2,1)S(1)} async-done(((bf16[4,32,1280]{2,1,0:T(8,128)(2,1)}), bf16[4,32,1280]{2,1,0:T(8,128)(2,1)S(1)}, u32[]{:S(2)}, u32[]{:S(2)}) %all-to-all-start.3) | async-done | bytes 327712 | tf_op jit(solution)/shard_map/all_to_all | solution.py:18
  83.7 0.3 convolution_convert_fusion.1
  84.0 0.3 convolution_convert_fusion
  84.4 0.1 pad_maximum_fusion
  84.4 9.8 %all_to_all.36 = bf16[4,64,1152]{2,1,0:T(8,128)(2,1)S(1)} all-to-all(bf16[4,64,1152]{2,1,0:T(8,128)(2,1)S(1)} %pad_maximum_fusion), channel_id=1, replica_groups=mesh['x'=4,'yh'=4,'yl'=2,'zh'=4,'zl'=2,'c'=2] {'x'}, dimensions={0} | all-to-all | bytes 1179648 | tf_op jit(solution)/shard_map/all_to_all | solution.py:18
  94.3 0.1 copy.32
  94.4 0.1 slice_reduce_fusion
  94.5 0.7 copy.33
  95.3 15.7 %all-to-all-start.5 = ((bf16[16,48,128]{2,1,0:T(8,128)(2,1)}), bf16[16,48,128]{2,1,0:T(8,128)(2,1)S(1)}, u32[]{:S(2)}, u32[]{:S(2)}) async-start(bf16[16,48,128]{2,1,0:T(8,128)(2,1)} %bitcast.16), calls=%async_computation.5 | async-start | bytes 393216 | tf_op jit(solution)/shard_map/all_to_all | solution.py:18
  110.9 0.6 select_reduce_fusion.index_ref
  111.5 9.7 %all-to-all-done.5.in_ref = bf16[16,48,128]{2,1,0:T(8,128)(2,1)S(1)} async-done(((bf16[16,48,128]{2,1,0:T(8,128)(2,1)}), bf16[16,48,128]{2,1,0:T(8,128)(2,1)S(1)}, u32[]{:S(2)}, u32[]{:S(2)}) %all-to-all-start.5) | async-done | bytes 196640 | tf_op jit(solution)/shard_map/all_to_all | solution.py:18
  121.2 1.5 shard_map.94
  122.8 3.5 %all-to-all-start.6 = ((bf16[16,3,48,128]{3,2,1,0:T(8,128)(2,1)}), bf16[16,3,48,128]{3,2,1,0:T(8,128)(2,1)S(1)}, u32[]{:S(2)}, u32[]{:S(2)}) async-start(bf16[16,3,48,128]{3,2,1,0:T(8,128)(2,1)} %bitcast.45), calls=%async_computation.6 | async-start | bytes 1179648 | tf_op jit(solution)/shard_map/all_to_all | solution.py:18
  126.3 0.0 copy-start
  126.3 0.0 copy-start.1
  126.3 0.2 compare_reduce_fusion
  126.5 0.5 convert_element_type.25.filled_ref
  127.0 17.5 %all-to-all-done.6 = bf16[16,3,48,128]{3,2,1,0:T(8,128)(2,1)S(1)} async-done(((bf16[16,3,48,128]{3,2,1,0:T(8,128)(2,1)}), bf16[16,3,48,128]{3,2,1,0:T(8,128)(2,1)S(1)}, u32[]{:S(2)}, u32[]{:S(2)}) %all-to-all-start.6) | async-done | bytes 589856 | tf_op jit(solution)/shard_map/all_to_all | solution.py:18
  144.6 0.2 copy.34
  144.8 0.3 reshape.84
  145.0 0.7 slice.34.left_ref
  145.8 0.0 copy-done
  145.8 1.1 add_select_fusion
  146.8 4.5 %all-gather.4.cloned.1.call-done = bf16[3,1024,1024]{2,1,0:T(8,128)(2,1)} async-done(((bf16[3,32,1024]{2,1,0:T(8,128)(2,1)}), bf16[3,1024,1024]{2,1,0:T(8,128)(2,1)}) %all-gather.4.cloned.1.call-update) | async-done | bytes 6291472 | tf_op jit(solution)/shard_map/all_gather | solution.py:93
  151.3 4.7 %shard_map.95 = bf16[3,32,1024]{2,1,0:T(8,128)(2,1)} custom-call(s32[3]{0:T(128)} %convert_element_type.25.filled_ref, bf16[3,32,1024]{2,1,0:T(8,128)(2,1)} %slice.34.left_ref, bf16[3,4,256,1024]{3,2,1,0:T(8,128)(2,1)} %bitcast.43), custom_call_target="tpu_custom_call" | custom-call | tf_op jit(solution)/shard_map/pallas_call | solution.py:65
  (19 shorter events, 0.3 us)
Async XLA Ops:
  7.2 28.4 %all-to-all-start = ((bf16[8,128,1024]{2,1,0:T(8,128)(2,1)}), bf16[8,128,1024]{2,1,0:T(8,128)(2,1)S(1)}, u32[]{:S(2)}, u32[]{:S(2)}) async-start(bf16[8,128,1024]{2,1,0:T(8,128)(2,1)} %bitcast.46), calls=%async_computation | async-start | bytes 4194304 | tf_op jit(solution)/shard_map/all_to_all | solution.py:18
  13.0 49.7 %all-gather.6.cloned.1.call-start = ((), (), s32[]{:S(2)}) async-start(), calls=%async_computation.8 | async-start | bytes 1769472 | tf_op jit(solution)/shard_map/all_gather | solution.py:89
  13.8 137.6 %all-gather.4.cloned.1.call-start = ((), (), s32[]{:S(2)}) async-start(), calls=%async_computation.7 | async-start | bytes 6488064 | tf_op jit(solution)/shard_map/all_gather | solution.py:93
  35.9 22.2 %copy-start.2 = (s32[16]{0:T(128)S(1)}, s32[16]{0:T(128)}, u32[]{:S(2)}) copy-start(s32[16]{0:T(128)} %param.8) | copy-start | bytes 196
  35.9 22.2 %copy-start.3 = (s32[16]{0:T(128)S(1)}, s32[16]{0:T(128)}, u32[]{:S(2)}) copy-start(s32[16]{0:T(128)} %param.9) | copy-start | bytes 196
  54.6 14.9 %all-to-all-start.2 = ((bf16[8,32,1024]{2,1,0:T(8,128)(2,1)}), bf16[8,32,1024]{2,1,0:T(8,128)(2,1)S(1)}, u32[]{:S(2)}, u32[]{:S(2)}) async-start(bf16[8,32,1024]{2,1,0:T(8,128)(2,1)} %broadcast_in_dim.53), calls=%async_computation.2 | async-start | bytes 1048576 | tf_op jit(solution)/shard_map/all_to_all | solution.py:18
  63.6 5.9 %collective-permute-start = (bf16[32,1024]{1,0:T(8,128)(2,1)S(1)}, bf16[32,1024]{1,0:T(8,128)(2,1)S(1)}, u32[]{:S(2)}, u32[]{:S(2)}) collective-permute-start(bf16[32,1024]{1,0:T(8,128)(2,1)S(1)} %get-tuple-element.15), channel_id=1, source_target_pairs={{0,2},{2,0},{1,3},{3,1},{4,6},{6,4},{5,7},{7,5},{8,10},{10,8},{9,1... | collective-permute-start | bytes 196616 | tf_op jit(solution)/shard_map/ppermute | solution.py:110
  70.4 13.2 %all-to-all-start.3 = ((bf16[4,32,1280]{2,1,0:T(8,128)(2,1)}), bf16[4,32,1280]{2,1,0:T(8,128)(2,1)S(1)}, u32[]{:S(2)}, u32[]{:S(2)}) async-start(bf16[4,32,1280]{2,1,0:T(8,128)(2,1)} %pad_maximum_fusion.1), calls=%async_computation.3 | async-start | bytes 655360 | tf_op jit(solution)/shard_map/all_to_all | solution.py:18
  95.3 26.0 %all-to-all-start.5 = ((bf16[16,48,128]{2,1,0:T(8,128)(2,1)}), bf16[16,48,128]{2,1,0:T(8,128)(2,1)S(1)}, u32[]{:S(2)}, u32[]{:S(2)}) async-start(bf16[16,48,128]{2,1,0:T(8,128)(2,1)} %bitcast.16), calls=%async_computation.5 | async-start | bytes 393216 | tf_op jit(solution)/shard_map/all_to_all | solution.py:18
  122.8 21.8 %all-to-all-start.6 = ((bf16[16,3,48,128]{3,2,1,0:T(8,128)(2,1)}), bf16[16,3,48,128]{3,2,1,0:T(8,128)(2,1)S(1)}, u32[]{:S(2)}, u32[]{:S(2)}) async-start(bf16[16,3,48,128]{3,2,1,0:T(8,128)(2,1)} %bitcast.45), calls=%async_computation.6 | async-start | bytes 1179648 | tf_op jit(solution)/shard_map/all_to_all | solution.py:18
  126.3 19.5 %copy-start = (f32[3,32,1024]{2,1,0:T(8,128)S(1)}, f32[3,32,1024]{2,1,0:T(8,128)}, u32[]{:S(2)}) copy-start(f32[3,32,1024]{2,1,0:T(8,128)} %param.11) | copy-start | bytes 1179652
  126.3 19.5 %copy-start.1 = (f32[3,32,1024]{2,1,0:T(8,128)S(1)}, f32[3,32,1024]{2,1,0:T(8,128)}, u32[]{:S(2)}) copy-start(f32[3,32,1024]{2,1,0:T(8,128)} %param.10) | copy-start | bytes 1179652
Sparse Core Ops, SparseCore 0:
  16.0 40.5 all-gather.5
  59.7 91.5 all-gather.3

commit v7 on v5

--- a/solution.py
+++ b/solution.py
@@ -106,7 +106,9 @@
     keeper = filled[:, None, None]
     new_left = jnp.where(keeper, 0.95 * left_stat + 0.05 * gl.astype(F32), left_stat)
     new_right = jnp.where(keeper, 0.95 * right_stat + 0.05 * gr.astype(F32), right_stat)
-    update = jnp.einsum("srn,snb->srb", mx, right_full, preferred_element_type=F32)
+    update = jnp.stack(
+        [jnp.dot(mx[i], right_full[i], preferred_element_type=F32) for i in range(slots)]
+    )
     update = jnp.where(keeper, update, 0.0).astype(BF16)
     return new_left, new_right, update
 

time: 164 us -> 166 us (1.012)
    dot_general x1 -> x3, matrix products: 4.65 us -> 6.18 us  [body(): jnp.dot(mx[i], right_full[i], preferred_element_type=F32)]
where the time goes in v7:
time: 166 us; the launch traced here: 165 us
  waiting for transfers between devices  63.7 us (38%)
  starting transfers between devices  39.1 us (24%)
  blocking collectives  27.6 us (17%)
  between operations  18.2 us (11%)
  matrix products  6.8 us (4%)
  other arithmetic  4.65 us (3%)
  local copies, waits for them, and re-layouts  3.48 us (2%)
    all_to_all x5, waiting for transfers between devices, swap(): return lax.all_to_all(value, axis, 0, 0, tiled=True)  55.9 us
    all_to_all x5, starting transfers between devices, swap(): return lax.all_to_all(value, axis, 0, 0, tiled=True)  35.1 us
    all_to_all x2, blocking collectives, swap(): return lax.all_to_all(value, axis, 0, 0, tiled=True)  27.6 us
    dot_general x3, matrix products, body(): jnp.dot(mx[i], right_full[i], preferred_element_type=F32)  6.18 us
    all_gather x1, waiting for transfers between devices, body(): lax.all_gather(right_root, ('x', 'yh', 'yl'), axis=1, tiled=True)  5.19 us
    ppermute x1, starting transfers between devices, body(): root = lax.ppermute(held(other), 'zl', [(i, i ^ 1) for i in range(NS)])  4 us
  transfers between devices with their start and end apart: 8, of which 6 were waited for; matrix products, arithmetic and copies ran while one was open for 5% of the time, Pallas kernels for 1%

profile of v7, /device:TPU:1, one launch (start us, length us, event | category | flops | bytes accessed | tf_op | source)
XLA Modules:
  0.0 165.2 jit_solution(10656720576242041744)
XLA Ops:
  7.2 5.9 %all-to-all-start = ((bf16[8,128,1024]{2,1,0:T(8,128)(2,1)}), bf16[8,128,1024]{2,1,0:T(8,128)(2,1)S(1)}, u32[]{:S(2)}, u32[]{:S(2)}) async-start(bf16[8,128,1024]{2,1,0:T(8,128)(2,1)} %bitcast.76), calls=%async_computation | async-start | bytes 4194304 | tf_op jit(solution)/shard_map/all_to_all | solution.py:18
  13.0 0.0 all-gather.6.cloned.1.call-start
  13.1 0.7 all-gather.6.cloned.1.call-update
  13.8 0.0 copy-start.2
  13.8 0.0 copy-start.3
  13.8 0.0 all-gather.4.cloned.1.call-start
  13.8 21.7 %all-to-all-done = bf16[8,128,1024]{2,1,0:T(8,128)(2,1)S(1)} async-done(((bf16[8,128,1024]{2,1,0:T(8,128)(2,1)}), bf16[8,128,1024]{2,1,0:T(8,128)(2,1)S(1)}, u32[]{:S(2)}, u32[]{:S(2)}) %all-to-all-start) | async-done | bytes 2097184 | tf_op jit(solution)/shard_map/all_to_all | solution.py:18
  35.5 0.4 reduce_sum.64
  35.9 0.0 all-gather.4.cloned.1.call-update
  35.9 17.7 %all_to_all.35 = bf16[4,32,1024]{2,1,0:T(8,128)(2,1)S(1)} all-to-all(bf16[4,32,1024]{2,1,0:T(8,128)(2,1)S(1)} %bitcast.78), channel_id=1, replica_groups=mesh['x'=4,'yh'=4,'yl'=2,'zh'=4,'zl'=2,'c'=2] {'yh'}, dimensions={0} | all-to-all | bytes 524288 | tf_op jit(solution)/shard_map/all_to_all | solution.py:18
  53.7 0.9 broadcast_in_dim.63
  54.6 3.5 %all-to-all-start.2 = ((bf16[8,32,1024]{2,1,0:T(8,128)(2,1)}), bf16[8,32,1024]{2,1,0:T(8,128)(2,1)S(1)}, u32[]{:S(2)}, u32[]{:S(2)}) async-start(bf16[8,32,1024]{2,1,0:T(8,128)(2,1)} %broadcast_in_dim.63), calls=%async_computation.2 | async-start | bytes 1048576 | tf_op jit(solution)/shard_map/all_to_all | solution.py:18
  58.1 0.0 copy-done.2
  58.1 0.0 copy-done.3
  58.2 0.6 fusion.9
  62.7 0.0 all-gather.6.cloned.1.call-done
  62.7 0.9 dynamic-slice_bitcast_fusion.2
  63.6 4.0 %collective-permute-start = (bf16[32,1024]{1,0:T(8,128)(2,1)S(1)}, bf16[32,1024]{1,0:T(8,128)(2,1)S(1)}, u32[]{:S(2)}, u32[]{:S(2)}) collective-permute-start(bf16[32,1024]{1,0:T(8,128)(2,1)S(1)} %get-tuple-element.15), channel_id=1, source_target_pairs={{0,2},{2,0},{1,3},{3,1},{4,6},{6,4},{5,7},{7,5},{8,10},{10,8},{9,1... | collective-permute-start | bytes 196616 | tf_op jit(solution)/shard_map/ppermute | solution.py:79
  67.6 1.9 %collective-permute-done = bf16[32,1024]{1,0:T(8,128)(2,1)S(1)} collective-permute-done((bf16[32,1024]{1,0:T(8,128)(2,1)S(1)}, bf16[32,1024]{1,0:T(8,128)(2,1)S(1)}, u32[]{:S(2)}, u32[]{:S(2)}) %collective-permute-start) | collective-permute-done | bytes 65568 | tf_op jit(solution)/shard_map/ppermute | solution.py:79
  69.5 0.0 all-to-all-done.2
  69.7 0.7 pad_maximum_fusion.1
  70.4 6.6 %all-to-all-start.3 = ((bf16[4,32,1280]{2,1,0:T(8,128)(2,1)}), bf16[4,32,1280]{2,1,0:T(8,128)(2,1)S(1)}, u32[]{:S(2)}, u32[]{:S(2)}) async-start(bf16[4,32,1280]{2,1,0:T(8,128)(2,1)} %pad_maximum_fusion.1), calls=%async_computation.3 | async-start | bytes 655360 | tf_op jit(solution)/shard_map/all_to_all | solution.py:18
  77.0 0.2 copy.30
  77.2 6.4 %all-to-all-done.3 = bf16[4,32,1280]{2,1,0:T(8,128)(2,1)S(1)} async-done(((bf16[4,32,1280]{2,1,0:T(8,128)(2,1)}), bf16[4,32,1280]{2,1,0:T(8,128)(2,1)S(1)}, u32[]{:S(2)}, u32[]{:S(2)}) %all-to-all-start.3) | async-done | bytes 327712 | tf_op jit(solution)/shard_map/all_to_all | solution.py:18
  83.6 0.3 convolution_convert_fusion.1
  84.0 0.3 convolution_convert_fusion
  84.3 0.1 pad_maximum_fusion
  84.4 9.9 %all_to_all.36 = bf16[4,64,1152]{2,1,0:T(8,128)(2,1)S(1)} all-to-all(bf16[4,64,1152]{2,1,0:T(8,128)(2,1)S(1)} %pad_maximum_fusion), channel_id=1, replica_groups=mesh['x'=4,'yh'=4,'yl'=2,'zh'=4,'zl'=2,'c'=2] {'x'}, dimensions={0} | all-to-all | bytes 1179648 | tf_op jit(solution)/shard_map/all_to_all | solution.py:18
  94.3 0.1 copy.33
  94.4 0.1 slice_reduce_fusion
  94.5 0.7 copy.34
  95.2 15.7 %all-to-all-start.5 = ((bf16[16,48,128]{2,1,0:T(8,128)(2,1)}), bf16[16,48,128]{2,1,0:T(8,128)(2,1)S(1)}, u32[]{:S(2)}, u32[]{:S(2)}) async-start(bf16[16,48,128]{2,1,0:T(8,128)(2,1)} %bitcast.16), calls=%async_computation.5 | async-start | bytes 393216 | tf_op jit(solution)/shard_map/all_to_all | solution.py:18
  110.9 0.6 select_reduce_fusion.index_ref
  111.5 9.7 %all-to-all-done.5.in_ref = bf16[16,48,128]{2,1,0:T(8,128)(2,1)S(1)} async-done(((bf16[16,48,128]{2,1,0:T(8,128)(2,1)}), bf16[16,48,128]{2,1,0:T(8,128)(2,1)S(1)}, u32[]{:S(2)}, u32[]{:S(2)}) %all-to-all-start.5) | async-done | bytes 196640 | tf_op jit(solution)/shard_map/all_to_all | solution.py:18
  121.2 1.5 shard_map.94
  122.8 3.5 %all-to-all-start.6 = ((bf16[16,3,48,128]{3,2,1,0:T(8,128)(2,1)}), bf16[16,3,48,128]{3,2,1,0:T(8,128)(2,1)S(1)}, u32[]{:S(2)}, u32[]{:S(2)}) async-start(bf16[16,3,48,128]{3,2,1,0:T(8,128)(2,1)} %bitcast.74), calls=%async_computation.6 | async-start | bytes 1179648 | tf_op jit(solution)/shard_map/all_to_all | solution.py:18
  126.3 0.2 compare_reduce_fusion
  126.5 18.1 %all-to-all-done.6 = bf16[16,3,48,128]{3,2,1,0:T(8,128)(2,1)S(1)} async-done(((bf16[16,3,48,128]{3,2,1,0:T(8,128)(2,1)}), bf16[16,3,48,128]{3,2,1,0:T(8,128)(2,1)S(1)}, u32[]{:S(2)}, u32[]{:S(2)}) %all-to-all-start.6) | async-done | bytes 589856 | tf_op jit(solution)/shard_map/all_to_all | solution.py:18
  144.5 0.2 copy.38
  144.8 0.3 reshape.81
  145.0 0.0 copy-done
  145.0 0.0 copy-done.1
  145.1 1.1 add_select_fusion
  146.1 5.2 %all-gather.4.cloned.1.call-done = bf16[3,1024,1024]{2,1,0:T(8,128)(2,1)} async-done(((bf16[3,32,1024]{2,1,0:T(8,128)(2,1)}), bf16[3,1024,1024]{2,1,0:T(8,128)(2,1)}) %all-gather.4.cloned.1.call-update) | async-done | bytes 6291472 | tf_op jit(solution)/shard_map/all_gather | solution.py:62
  151.3 2.1 %fusion.3 = bf16[1,32,1024]{2,1,0:T(8,128)(2,1)S(1)} fusion(bf16[3,1024,1024]{2,1,0:T(8,128)(2,1)} %all-gather.4.cloned.1.call-done, bf16[3,96,1024]{2,1,0:T(8,128)(2,1)S(1)} %reshape.81), kind=kOutput, calls=%fused_computation.7 | convolution fusion | flops 67108864 | bytes 2228224 | tf_op jit(solution)/shard_map/dot_general | solution.py:110
  153.4 2.1 %fusion.4 = bf16[1,32,1024]{2,1,0:T(8,128)(2,1)S(1)} fusion(bf16[3,1024,1024]{2,1,0:T(8,128)(2,1)} %all-gather.4.cloned.1.call-done, bf16[3,96,1024]{2,1,0:T(8,128)(2,1)S(1)} %reshape.81), kind=kOutput, calls=%fused_computation.8 | convolution fusion | flops 67108864 | bytes 2228224 | tf_op jit(solution)/shard_map/dot_general | solution.py:110
  155.5 2.1 %fusion.5 = bf16[1,32,1024]{2,1,0:T(8,128)(2,1)S(1)} fusion(bf16[3,1024,1024]{2,1,0:T(8,128)(2,1)} %all-gather.4.cloned.1.call-done, bf16[3,96,1024]{2,1,0:T(8,128)(2,1)S(1)} %reshape.81), kind=kOutput, calls=%fused_computation.9 | convolution fusion | flops 67108864 | bytes 2228224 | tf_op jit(solution)/shard_map/dot_general | solution.py:110
  157.5 0.8 fusion.6
  (20 shorter events, 0.3 us)
Async XLA Ops:
  7.2 28.4 %all-to-all-start = ((bf16[8,128,1024]{2,1,0:T(8,128)(2,1)}), bf16[8,128,1024]{2,1,0:T(8,128)(2,1)S(1)}, u32[]{:S(2)}, u32[]{:S(2)}) async-start(bf16[8,128,1024]{2,1,0:T(8,128)(2,1)} %bitcast.76), calls=%async_computation | async-start | bytes 4194304 | tf_op jit(solution)/shard_map/all_to_all | solution.py:18
  13.0 49.7 %all-gather.6.cloned.1.call-start = ((), (), s32[]{:S(2)}) async-start(), calls=%async_computation.8 | async-start | bytes 1769472 | tf_op jit(solution)/shard_map/all_gather | solution.py:58
  13.8 44.4 %copy-start.2 = (s32[16]{0:T(128)S(1)}, s32[16]{0:T(128)}, u32[]{:S(2)}) copy-start(s32[16]{0:T(128)} %param.8) | copy-start | bytes 196
  13.8 44.3 %copy-start.3 = (s32[16]{0:T(128)S(1)}, s32[16]{0:T(128)}, u32[]{:S(2)}) copy-start(s32[16]{0:T(128)} %param.9) | copy-start | bytes 196
  13.8 137.5 %all-gather.4.cloned.1.call-start = ((), (), s32[]{:S(2)}) async-start(), calls=%async_computation.7 | async-start | bytes 6488064 | tf_op jit(solution)/shard_map/all_gather | solution.py:62
  54.6 14.9 %all-to-all-start.2 = ((bf16[8,32,1024]{2,1,0:T(8,128)(2,1)}), bf16[8,32,1024]{2,1,0:T(8,128)(2,1)S(1)}, u32[]{:S(2)}, u32[]{:S(2)}) async-start(bf16[8,32,1024]{2,1,0:T(8,128)(2,1)} %broadcast_in_dim.63), calls=%async_computation.2 | async-start | bytes 1048576 | tf_op jit(solution)/shard_map/all_to_all | solution.py:18
  63.6 5.9 %collective-permute-start = (bf16[32,1024]{1,0:T(8,128)(2,1)S(1)}, bf16[32,1024]{1,0:T(8,128)(2,1)S(1)}, u32[]{:S(2)}, u32[]{:S(2)}) collective-permute-start(bf16[32,1024]{1,0:T(8,128)(2,1)S(1)} %get-tuple-element.15), channel_id=1, source_target_pairs={{0,2},{2,0},{1,3},{3,1},{4,6},{6,4},{5,7},{7,5},{8,10},{10,8},{9,1... | collective-permute-start | bytes 196616 | tf_op jit(solution)/shard_map/ppermute | solution.py:79
  70.4 13.2 %all-to-all-start.3 = ((bf16[4,32,1280]{2,1,0:T(8,128)(2,1)}), bf16[4,32,1280]{2,1,0:T(8,128)(2,1)S(1)}, u32[]{:S(2)}, u32[]{:S(2)}) async-start(bf16[4,32,1280]{2,1,0:T(8,128)(2,1)} %pad_maximum_fusion.1), calls=%async_computation.3 | async-start | bytes 655360 | tf_op jit(solution)/shard_map/all_to_all | solution.py:18
  95.2 26.0 %all-to-all-start.5 = ((bf16[16,48,128]{2,1,0:T(8,128)(2,1)}), bf16[16,48,128]{2,1,0:T(8,128)(2,1)S(1)}, u32[]{:S(2)}, u32[]{:S(2)}) async-start(bf16[16,48,128]{2,1,0:T(8,128)(2,1)} %bitcast.16), calls=%async_computation.5 | async-start | bytes 393216 | tf_op jit(solution)/shard_map/all_to_all | solution.py:18
  111.5 33.5 %copy-start = (f32[3,32,1024]{2,1,0:T(8,128)S(1)}, f32[3,32,1024]{2,1,0:T(8,128)}, u32[]{:S(2)}) copy-start(f32[3,32,1024]{2,1,0:T(8,128)} %param.11) | copy-start | bytes 1179652
  111.5 33.5 %copy-start.1 = (f32[3,32,1024]{2,1,0:T(8,128)S(1)}, f32[3,32,1024]{2,1,0:T(8,128)}, u32[]{:S(2)}) copy-start(f32[3,32,1024]{2,1,0:T(8,128)} %param.10) | copy-start | bytes 1179652
  122.8 21.8 %all-to-all-start.6 = ((bf16[16,3,48,128]{3,2,1,0:T(8,128)(2,1)}), bf16[16,3,48,128]{3,2,1,0:T(8,128)(2,1)S(1)}, u32[]{:S(2)}, u32[]{:S(2)}) async-start(bf16[16,3,48,128]{3,2,1,0:T(8,128)(2,1)} %bitcast.74), calls=%async_computation.6 | async-start | bytes 1179648 | tf_op jit(solution)/shard_map/all_to_all | solution.py:18
Sparse Core Ops, SparseCore 0:
  16.0 40.5 all-gather.5
  59.7 91.5 all-gather.3

commit v8 on v5

--- a/solution.py
+++ b/solution.py
@@ -55,7 +55,7 @@
     block_of = jnp.sum(jnp.where(named, jnp.arange(MP, dtype=jnp.int32)[None, :], 0), axis=1)
     filled = jnp.any(target[None, :] == (here * slots + jnp.arange(slots, dtype=jnp.int32))[:, None], axis=1)
 
-    roots = lax.all_gather(left_root, ("zh", "c"), axis=0)
+    roots = lax.all_gather(left_root, ("c", "zh"), axis=0)
 
     part = add_up(swap(grad_parts[0].reshape(NX * NL, ix_panel // NL, b), ("x", "yl")))
     right_root, part = lax.optimization_barrier((right_root, part))
@@ -65,7 +65,7 @@
     panel = share(chunk, ("yl", "yh"), NY).reshape(ix_panel, b)
 
     bands = jnp.arange(MP, dtype=jnp.int32)
-    place = ((owner >> 2) * NC + (owner & 1)) * slots + slot
+    place = ((owner & 1) * (NZ // NS) + (owner >> 2)) * slots + slot
     place = place + jnp.where(((owner ^ bands) & NC) == 0, 0, MP * slots)
     mine = jnp.sum(jnp.where(bands == here, place, 0))
     other = jnp.sum(jnp.where(bands == here ^ NC, place, 0))

time: 164 us -> 164 us (level)
  no operation moved by 1% of the time
where the time goes in v8:
time: 164 us; the launch traced here: 163 us
  waiting for transfers between devices  63.8 us (39%)
  starting transfers between devices  39.2 us (24%)
  blocking collectives  27.6 us (17%)
  between operations  18.2 us (11%)
  matrix products  5.27 us (3%)
  other arithmetic  3.83 us (2%)
  local copies, waits for them, and re-layouts  3.48 us (2%)
    all_to_all x5, waiting for transfers between devices, swap(): return lax.all_to_all(value, axis, 0, 0, tiled=True)  55.9 us
    all_to_all x5, starting transfers between devices, swap(): return lax.all_to_all(value, axis, 0, 0, tiled=True)  35.1 us
    all_to_all x2, blocking collectives, swap(): return lax.all_to_all(value, axis, 0, 0, tiled=True)  27.6 us
    all_gather x1, waiting for transfers between devices, body(): lax.all_gather(right_root, ('x', 'yh', 'yl'), axis=1, tiled=True)  5.24 us
    dot_general x1, matrix products, body(): jnp.einsum('srn,snb->srb', mx, right_full, preferred_element_type=F32)  4.65 us
    ppermute x1, starting transfers between devices, body(): root = lax.ppermute(held(other), 'zl', [(i, i ^ 1) for i in range(NS)])  4 us
  transfers between devices with their start and end apart: 8, of which 6 were waited for; matrix products, arithmetic and copies ran while one was open for 5% of the time, Pallas kernels for 1%

profile of v8, /device:TPU:1, one launch (start us, length us, event | category | flops | bytes accessed | tf_op | source)
XLA Modules:
  0.0 162.9 jit_solution(12974338267435068823)
XLA Ops:
  7.2 5.9 %all-to-all-start = ((bf16[8,128,1024]{2,1,0:T(8,128)(2,1)}), bf16[8,128,1024]{2,1,0:T(8,128)(2,1)S(1)}, u32[]{:S(2)}, u32[]{:S(2)}) async-start(bf16[8,128,1024]{2,1,0:T(8,128)(2,1)} %bitcast.47), calls=%async_computation | async-start | bytes 4194304 | tf_op jit(solution)/shard_map/all_to_all | solution.py:18
  13.0 0.0 all-gather.6.cloned.1.call-start
  13.1 0.7 all-gather.6.cloned.1.call-update
  13.8 0.0 copy-start.2
  13.8 0.0 copy-start.3
  13.8 0.0 all-gather.4.cloned.1.call-start
  13.8 21.7 %all-to-all-done = bf16[8,128,1024]{2,1,0:T(8,128)(2,1)S(1)} async-done(((bf16[8,128,1024]{2,1,0:T(8,128)(2,1)}), bf16[8,128,1024]{2,1,0:T(8,128)(2,1)S(1)}, u32[]{:S(2)}, u32[]{:S(2)}) %all-to-all-start) | async-done | bytes 2097184 | tf_op jit(solution)/shard_map/all_to_all | solution.py:18
  35.5 0.4 reduce_sum.64
  35.9 0.0 all-gather.4.cloned.1.call-update
  35.9 17.7 %all_to_all.35 = bf16[4,32,1024]{2,1,0:T(8,128)(2,1)S(1)} all-to-all(bf16[4,32,1024]{2,1,0:T(8,128)(2,1)S(1)} %bitcast.49), channel_id=1, replica_groups=mesh['x'=4,'yh'=4,'yl'=2,'zh'=4,'zl'=2,'c'=2] {'yh'}, dimensions={0} | all-to-all | bytes 524288 | tf_op jit(solution)/shard_map/all_to_all | solution.py:18
  53.7 0.9 broadcast_in_dim.63
  54.6 3.5 %all-to-all-start.2 = ((bf16[8,32,1024]{2,1,0:T(8,128)(2,1)}), bf16[8,32,1024]{2,1,0:T(8,128)(2,1)S(1)}, u32[]{:S(2)}, u32[]{:S(2)}) async-start(bf16[8,32,1024]{2,1,0:T(8,128)(2,1)} %broadcast_in_dim.63), calls=%async_computation.2 | async-start | bytes 1048576 | tf_op jit(solution)/shard_map/all_to_all | solution.py:18
  58.1 0.0 copy-done.2
  58.1 0.0 copy-done.3
  58.1 0.6 fusion.4
  62.7 0.0 all-gather.6.cloned.1.call-done
  62.7 0.9 dynamic-slice_bitcast_fusion.2
  63.6 4.0 %collective-permute-start = (bf16[32,1024]{1,0:T(8,128)(2,1)S(1)}, bf16[32,1024]{1,0:T(8,128)(2,1)S(1)}, u32[]{:S(2)}, u32[]{:S(2)}) collective-permute-start(bf16[32,1024]{1,0:T(8,128)(2,1)S(1)} %get-tuple-element.15), channel_id=1, source_target_pairs={{0,2},{2,0},{1,3},{3,1},{4,6},{6,4},{5,7},{7,5},{8,10},{10,8},{9,1... | collective-permute-start | bytes 196616 | tf_op jit(solution)/shard_map/ppermute | solution.py:79
  67.6 1.9 %collective-permute-done = bf16[32,1024]{1,0:T(8,128)(2,1)S(1)} collective-permute-done((bf16[32,1024]{1,0:T(8,128)(2,1)S(1)}, bf16[32,1024]{1,0:T(8,128)(2,1)S(1)}, u32[]{:S(2)}, u32[]{:S(2)}) %collective-permute-start) | collective-permute-done | bytes 65568 | tf_op jit(solution)/shard_map/ppermute | solution.py:79
  69.5 0.0 all-to-all-done.2
  69.6 0.7 pad_maximum_fusion.1
  70.4 6.6 %all-to-all-start.3 = ((bf16[4,32,1280]{2,1,0:T(8,128)(2,1)}), bf16[4,32,1280]{2,1,0:T(8,128)(2,1)S(1)}, u32[]{:S(2)}, u32[]{:S(2)}) async-start(bf16[4,32,1280]{2,1,0:T(8,128)(2,1)} %pad_maximum_fusion.1), calls=%async_computation.3 | async-start | bytes 655360 | tf_op jit(solution)/shard_map/all_to_all | solution.py:18
  77.0 0.2 copy.30
  77.2 6.4 %all-to-all-done.3 = bf16[4,32,1280]{2,1,0:T(8,128)(2,1)S(1)} async-done(((bf16[4,32,1280]{2,1,0:T(8,128)(2,1)}), bf16[4,32,1280]{2,1,0:T(8,128)(2,1)S(1)}, u32[]{:S(2)}, u32[]{:S(2)}) %all-to-all-start.3) | async-done | bytes 327712 | tf_op jit(solution)/shard_map/all_to_all | solution.py:18
  83.6 0.3 convolution_convert_fusion.1
  84.0 0.3 convolution_convert_fusion
  84.3 0.1 pad_maximum_fusion
  84.3 9.9 %all_to_all.36 = bf16[4,64,1152]{2,1,0:T(8,128)(2,1)S(1)} all-to-all(bf16[4,64,1152]{2,1,0:T(8,128)(2,1)S(1)} %pad_maximum_fusion), channel_id=1, replica_groups=mesh['x'=4,'yh'=4,'yl'=2,'zh'=4,'zl'=2,'c'=2] {'x'}, dimensions={0} | all-to-all | bytes 1179648 | tf_op jit(solution)/shard_map/all_to_all | solution.py:18
  94.2 0.1 copy.33
  94.3 0.1 slice_reduce_fusion
  94.5 0.7 copy.34
  95.2 15.7 %all-to-all-start.5 = ((bf16[16,48,128]{2,1,0:T(8,128)(2,1)}), bf16[16,48,128]{2,1,0:T(8,128)(2,1)S(1)}, u32[]{:S(2)}, u32[]{:S(2)}) async-start(bf16[16,48,128]{2,1,0:T(8,128)(2,1)} %bitcast.16), calls=%async_computation.5 | async-start | bytes 393216 | tf_op jit(solution)/shard_map/all_to_all | solution.py:18
  110.9 0.6 select_reduce_fusion.index_ref
  111.5 0.0 copy-start
  111.5 0.0 copy-start.1
  111.5 9.7 %all-to-all-done.5.in_ref = bf16[16,48,128]{2,1,0:T(8,128)(2,1)S(1)} async-done(((bf16[16,48,128]{2,1,0:T(8,128)(2,1)}), bf16[16,48,128]{2,1,0:T(8,128)(2,1)S(1)}, u32[]{:S(2)}, u32[]{:S(2)}) %all-to-all-start.5) | async-done | bytes 196640 | tf_op jit(solution)/shard_map/all_to_all | solution.py:18
  121.2 1.5 shard_map.94
  122.8 3.5 %all-to-all-start.6 = ((bf16[16,3,48,128]{3,2,1,0:T(8,128)(2,1)}), bf16[16,3,48,128]{3,2,1,0:T(8,128)(2,1)S(1)}, u32[]{:S(2)}, u32[]{:S(2)}) async-start(bf16[16,3,48,128]{3,2,1,0:T(8,128)(2,1)} %bitcast.45), calls=%async_computation.6 | async-start | bytes 1179648 | tf_op jit(solution)/shard_map/all_to_all | solution.py:18
  126.3 0.2 compare_reduce_fusion
  126.5 18.1 %all-to-all-done.6 = bf16[16,3,48,128]{3,2,1,0:T(8,128)(2,1)S(1)} async-done(((bf16[16,3,48,128]{3,2,1,0:T(8,128)(2,1)}), bf16[16,3,48,128]{3,2,1,0:T(8,128)(2,1)S(1)}, u32[]{:S(2)}, u32[]{:S(2)}) %all-to-all-start.6) | async-done | bytes 589856 | tf_op jit(solution)/shard_map/all_to_all | solution.py:18
  144.5 0.2 copy.38
  144.8 0.3 reshape.81
  145.0 0.0 copy-done
  145.0 0.0 copy-done.1
  145.0 1.1 add_select_fusion
  146.1 5.2 %all-gather.4.cloned.1.call-done = bf16[3,1024,1024]{2,1,0:T(8,128)(2,1)} async-done(((bf16[3,32,1024]{2,1,0:T(8,128)(2,1)}), bf16[3,1024,1024]{2,1,0:T(8,128)(2,1)}) %all-gather.4.cloned.1.call-update) | async-done | bytes 6291472 | tf_op jit(solution)/shard_map/all_gather | solution.py:62
  151.4 4.7 %fusion = bf16[3,32,1024]{2,1,0:T(8,128)(2,1)} fusion(bf16[3,1024,1024]{2,1,0:T(8,128)(2,1)} %all-gather.4.cloned.1.call-done, bf16[3,96,1024]{2,1,0:T(8,128)(2,1)S(1)} %reshape.81, pred[3]{0:T(512)(128)(4,1)S(1)} %compare_reduce_fusion), kind=kOutput, calls=%fused_computation.2 | convolution fusion | flops 201523200 | bytes 6685184 | tf_op jit(solution)/shard_map/srn,snb->srb/dot_general | solution.py:109
  (18 shorter events, 0.3 us)
Async XLA Ops:
  7.2 28.4 %all-to-all-start = ((bf16[8,128,1024]{2,1,0:T(8,128)(2,1)}), bf16[8,128,1024]{2,1,0:T(8,128)(2,1)S(1)}, u32[]{:S(2)}, u32[]{:S(2)}) async-start(bf16[8,128,1024]{2,1,0:T(8,128)(2,1)} %bitcast.47), calls=%async_computation | async-start | bytes 4194304 | tf_op jit(solution)/shard_map/all_to_all | solution.py:18
  13.0 49.7 %all-gather.6.cloned.1.call-start = ((), (), s32[]{:S(2)}) async-start(), calls=%async_computation.8 | async-start | bytes 1769472 | tf_op jit(solution)/shard_map/all_gather | solution.py:58
  13.8 44.3 %copy-start.2 = (s32[16]{0:T(128)S(1)}, s32[16]{0:T(128)}, u32[]{:S(2)}) copy-start(s32[16]{0:T(128)} %param.8) | copy-start | bytes 196
  13.8 44.3 %copy-start.3 = (s32[16]{0:T(128)S(1)}, s32[16]{0:T(128)}, u32[]{:S(2)}) copy-start(s32[16]{0:T(128)} %param.9) | copy-start | bytes 196
  13.8 137.6 %all-gather.4.cloned.1.call-start = ((), (), s32[]{:S(2)}) async-start(), calls=%async_computation.7 | async-start | bytes 6488064 | tf_op jit(solution)/shard_map/all_gather | solution.py:62
  54.6 14.9 %all-to-all-start.2 = ((bf16[8,32,1024]{2,1,0:T(8,128)(2,1)}), bf16[8,32,1024]{2,1,0:T(8,128)(2,1)S(1)}, u32[]{:S(2)}, u32[]{:S(2)}) async-start(bf16[8,32,1024]{2,1,0:T(8,128)(2,1)} %broadcast_in_dim.63), calls=%async_computation.2 | async-start | bytes 1048576 | tf_op jit(solution)/shard_map/all_to_all | solution.py:18
  63.6 5.9 %collective-permute-start = (bf16[32,1024]{1,0:T(8,128)(2,1)S(1)}, bf16[32,1024]{1,0:T(8,128)(2,1)S(1)}, u32[]{:S(2)}, u32[]{:S(2)}) collective-permute-start(bf16[32,1024]{1,0:T(8,128)(2,1)S(1)} %get-tuple-element.15), channel_id=1, source_target_pairs={{0,2},{2,0},{1,3},{3,1},{4,6},{6,4},{5,7},{7,5},{8,10},{10,8},{9,1... | collective-permute-start | bytes 196616 | tf_op jit(solution)/shard_map/ppermute | solution.py:79
  70.4 13.2 %all-to-all-start.3 = ((bf16[4,32,1280]{2,1,0:T(8,128)(2,1)}), bf16[4,32,1280]{2,1,0:T(8,128)(2,1)S(1)}, u32[]{:S(2)}, u32[]{:S(2)}) async-start(bf16[4,32,1280]{2,1,0:T(8,128)(2,1)} %pad_maximum_fusion.1), calls=%async_computation.3 | async-start | bytes 655360 | tf_op jit(solution)/shard_map/all_to_all | solution.py:18
  95.2 26.0 %all-to-all-start.5 = ((bf16[16,48,128]{2,1,0:T(8,128)(2,1)}), bf16[16,48,128]{2,1,0:T(8,128)(2,1)S(1)}, u32[]{:S(2)}, u32[]{:S(2)}) async-start(bf16[16,48,128]{2,1,0:T(8,128)(2,1)} %bitcast.16), calls=%async_computation.5 | async-start | bytes 393216 | tf_op jit(solution)/shard_map/all_to_all | solution.py:18
  111.5 33.5 %copy-start = (f32[3,32,1024]{2,1,0:T(8,128)S(1)}, f32[3,32,1024]{2,1,0:T(8,128)}, u32[]{:S(2)}) copy-start(f32[3,32,1024]{2,1,0:T(8,128)} %param.11) | copy-start | bytes 1179652
  111.5 33.5 %copy-start.1 = (f32[3,32,1024]{2,1,0:T(8,128)S(1)}, f32[3,32,1024]{2,1,0:T(8,128)}, u32[]{:S(2)}) copy-start(f32[3,32,1024]{2,1,0:T(8,128)} %param.10) | copy-start | bytes 1179652
  122.8 21.8 %all-to-all-start.6 = ((bf16[16,3,48,128]{3,2,1,0:T(8,128)(2,1)}), bf16[16,3,48,128]{3,2,1,0:T(8,128)(2,1)S(1)}, u32[]{:S(2)}, u32[]{:S(2)}) async-start(bf16[16,3,48,128]{3,2,1,0:T(8,128)(2,1)} %bitcast.45), calls=%async_computation.6 | async-start | bytes 1179648 | tf_op jit(solution)/shard_map/all_to_all | solution.py:18
Sparse Core Ops, SparseCore 0:
  16.0 40.5 all-gather.5
  59.8 91.5 all-gather.3
